TPU v7x, 32 devices: a whole 2x2x4 slice. The times are simulated.
32 devices in a mesh: band: 4 (over y, x), dom: 8 (over z, core).
Axes of the slice: x: 2, y: 2, z: 4, core: 2. Of those that a mesh axis runs over, the one named last changes fastest.
Arguments:
- orbitals: float32 [16, 32, 32, 1024], P('dom', None, None, 'band'), may hold values from -6 to 6
- potential: float32 [16, 32, 32], P('dom'), may hold values from -2 to 2
- projectors: float32 [1024, 8, 256], P('dom'), may hold values from -0.375 to 0.375
- tile_cells: int32 [1024, 256], P('dom'), may hold values from 0 to 2047
- tile_atom: int32 [1024], replicated, may hold values from -1 to 63, as said below
- atom_owner: int32 [64], replicated, may hold values from 0 to 63, as said below
- coupling: float32 [64, 8, 8], P('dom'), may hold values from -2 to 2
- rotation: float32 [1024, 1024], P(None, 'band'), may hold values from -0.1875 to 0.1875
Outputs:
- rotated_orbitals: float32 [16, 32, 32, 1024], P('dom', None, None, 'band')
- rotated_applied: float32 [16, 32, 32, 1024], P('dom', None, None, 'band')
Inputs may be any that keep to these rules, and one draw needn't show every extreme that they name: `tile_atom`: tile slots come in blocks of 128, one block a domain; in each block the used slots come first, at least half of them are used, and some block is full. An atom a is owned by domain atom_owner[a] // 8. The tiles of one domain name atoms of any one owning domain at most 32 times, and some owning domain is named exactly 32 times by every domain. `atom_owner`: each row of the coupling table belongs to exactly one atom.
All inputs are finite; a program needn't handle non-finite values.
Results may differ from a plain program's by a relative error of at most 0.000071.
Values sent between devices are 32-bit elements; how exact they have to be, the bound alone decides.
A program may use at most 128 MiB of HBM per device.

v0:
```python
import jax
import jax.numpy as jnp
from jax import lax
from jax.sharding import PartitionSpec as P


def padded_2(cells, sides, width):
    for axis, dim in sides:
        count = lax.axis_size(axis)
        head = lax.slice_in_dim(cells, 0, width, axis=dim)
        tail = lax.slice_in_dim(cells, cells.shape[dim] - width, cells.shape[dim], axis=dim)
        cells = jnp.concatenate(
            [
                lax.ppermute(tail, axis, [(i, (i + 1) % count) for i in range(count)]),
                cells,
                lax.ppermute(head, axis, [((i + 1) % count, i) for i in range(count)]),
            ],
            axis=dim,
        )
    return cells


def owner_rows(atom_ids, atom_owner):
    match = atom_ids[..., None] == jnp.arange(atom_owner.shape[0], dtype=jnp.int32)
    found_rows = jnp.sum(jnp.where(match, atom_owner, 0), axis=-1)
    return jnp.where(atom_ids >= 0, found_rows, -1)


def body(orbitals, potential, projectors, tile_cells, tile_atom, atom_owner, coupling, rotation):
    plane_count, rows_y, rows_z, band_count = orbitals.shape
    cell_count = plane_count * rows_y * rows_z
    entry_count, proj_count, tile_size = projectors.shape
    atom_total = atom_owner.shape[0]
    domain_index = lax.axis_index("dom")
    padded = padded_2(orbitals, (("dom", 0),), 1)
    beside = padded[2:] + padded[:-2]
    beside = beside + jnp.roll(orbitals, 1, 1) + jnp.roll(orbitals, -1, 1)
    beside = beside + jnp.roll(orbitals, 1, 2) + jnp.roll(orbitals, -1, 2)
    applied_local = (3.0 + potential[..., None]) * orbitals - 0.5 * beside
    flat_field = orbitals.reshape(cell_count, band_count)
    block_size = min(16, entry_count)
    block_count = entry_count // block_size
    cell_blocks = tile_cells.reshape(block_count, block_size, tile_size)
    value_blocks = projectors.reshape(block_count, block_size, proj_count, tile_size)
    cell_ids = jnp.arange(cell_count, dtype=jnp.int32)

    def densify(inputs):
        tile_index, values = inputs
        one_hot = (tile_index[..., None] == cell_ids).astype(jnp.float32)
        return jnp.einsum("ekt,etc->ekc", values, one_hot, precision=lax.Precision.HIGHEST)

    dense_proj = lax.map(densify, (cell_blocks, value_blocks)).reshape(
        entry_count * proj_count, cell_count
    )
    partials = jnp.dot(
        dense_proj, flat_field, precision=lax.Precision.HIGHEST, preferred_element_type=jnp.float32
    )
    partials = partials.reshape(entry_count, proj_count, band_count)
    my_atoms = lax.dynamic_slice_in_dim(tile_atom, domain_index * entry_count, entry_count)
    my_rows = owner_rows(my_atoms, atom_owner)
    row_match = (my_rows[:, None] == jnp.arange(atom_total, dtype=jnp.int32)[None, :]).astype(
        jnp.float32
    )
    columns = row_match
    owned_sums = lax.psum_scatter(
        jnp.einsum("ea,ekb->akb", columns, partials, precision=lax.Precision.HIGHEST),
        "dom",
        scatter_dimension=0,
        tiled=True,
    )
    scaled = jnp.einsum("akj,ajb->akb", coupling, owned_sums, precision=lax.Precision.HIGHEST)
    columns = row_match
    returned = jnp.einsum(
        "ea,akb->ekb",
        columns,
        lax.all_gather(scaled, "dom", axis=0, tiled=True),
        precision=lax.Precision.HIGHEST,
    )
    returned_rows = returned.reshape(entry_count * proj_count, band_count)
    applied_far = jnp.einsum(
        "rc,rb->cb", dense_proj, returned_rows, precision=lax.Precision.HIGHEST
    )
    applied = applied_local + applied_far.reshape(orbitals.shape)
    first_sum = jnp.einsum(
        "xyzb,bc->xyzc",
        lax.all_gather(orbitals, "band", axis=3, tiled=True),
        rotation,
        precision=lax.Precision.HIGHEST,
    )
    second_sum = jnp.einsum(
        "xyzb,bc->xyzc",
        lax.all_gather(applied, "band", axis=3, tiled=True),
        rotation,
        precision=lax.Precision.HIGHEST,
    )
    return (first_sum, second_sum)


def solution(mesh):
    return jax.shard_map(
        body,
        mesh=mesh,
        in_specs=(
            P("dom", None, None, "band"),
            P("dom", None, None),
            P("dom", None, None),
            P("dom", None),
            P(),
            P(),
            P("dom", None, None),
            P(None, "band"),
        ),
        out_specs=(P("dom", None, None, "band"), P("dom", None, None, "band")),
        check_vma=False,
    )
```

profile of v0, /device:TPU:0, one launch (start us, length us, event | category | flops | bytes accessed | tf_op | source)
XLA Modules:
  0.0 325.3 jit_solution(13490650550880753013)
XLA Ops:
  8.0 0.0 copy-start
  8.0 0.0 reduce-scatter.2.cloned.1.call-start
  8.1 0.8 dynamic_slice.11
  8.9 0.7 select_reduce_fusion
  9.7 0.8 compare_select_fusion
  10.4 0.0 copy-start.1
  10.4 104.6 %while.11 = (s32[]{:T(128)}, f32[8,16,8,2048]{3,2,1,0:T(8,128)}, f32[8,16,8,256]{3,2,1,0:T(8,128)}, s32[8,16,256]{2,1,0:T(8,128)}, s32[]{:T(128)}) while((s32[]{:T(128)}, f32[8,16,8,2048]{3,2,1,0:T(8,128)}, f32[8,16,8,256]{3,2,1,0:T(8,128)}, s32[8,16,256]{2,1,0:T(8,128)}, s32[]{:T(128)}) %tuple.40), condition=%wide.region_1.2_spmd.clone, body=%wide.region_0.1_spmd.clone.sunk | while | flops 813694976 | bytes 1229889 | solution.py:52
  10.4 0.9 dynamic-slice_bitcast_fusion.2
  11.3 12.3 %fusion.48 = f32[8,16,8,2048]{3,2,1,0:T(8,128)} fusion(f32[8,16,8,2048]{3,2,1,0:T(8,128)} %get-tuple-element.89, s32[]{:T(128)} %get-tuple-element.88, s32[16,256]{1,0:T(8,128)S(1)} %dynamic-slice_bitcast_fusion.2, f32[8,16,8,256]{3,2,1,0:T(8,128)} %get-tuple-element.95), kind=kOutput, calls=%fused_computation.5.clone.1 | convolution fusion | flops 813694976 | bytes 1197056 | tf_op jit(solution)/shard_map/while/body/eval_jaxpr/ekt,etc->ekc/dot_general | solution.py:50
  23.6 0.7 dynamic-slice_bitcast_fusion.2
  24.3 12.3 %fusion.48 = f32[8,16,8,2048]{3,2,1,0:T(8,128)} fusion(f32[8,16,8,2048]{3,2,1,0:T(8,128)} %get-tuple-element.89, s32[]{:T(128)} %get-tuple-element.88, s32[16,256]{1,0:T(8,128)S(1)} %dynamic-slice_bitcast_fusion.2, f32[8,16,8,256]{3,2,1,0:T(8,128)} %get-tuple-element.95), kind=kOutput, calls=%fused_computation.5.clone.1 | convolution fusion | flops 813694976 | bytes 1197056 | tf_op jit(solution)/shard_map/while/body/eval_jaxpr/ekt,etc->ekc/dot_general | solution.py:50
  36.7 0.7 dynamic-slice_bitcast_fusion.2
  37.4 12.3 %fusion.48 = f32[8,16,8,2048]{3,2,1,0:T(8,128)} fusion(f32[8,16,8,2048]{3,2,1,0:T(8,128)} %get-tuple-element.89, s32[]{:T(128)} %get-tuple-element.88, s32[16,256]{1,0:T(8,128)S(1)} %dynamic-slice_bitcast_fusion.2, f32[8,16,8,256]{3,2,1,0:T(8,128)} %get-tuple-element.95), kind=kOutput, calls=%fused_computation.5.clone.1 | convolution fusion | flops 813694976 | bytes 1197056 | tf_op jit(solution)/shard_map/while/body/eval_jaxpr/ekt,etc->ekc/dot_general | solution.py:50
  49.7 0.7 dynamic-slice_bitcast_fusion.2
  50.4 12.3 %fusion.48 = f32[8,16,8,2048]{3,2,1,0:T(8,128)} fusion(f32[8,16,8,2048]{3,2,1,0:T(8,128)} %get-tuple-element.89, s32[]{:T(128)} %get-tuple-element.88, s32[16,256]{1,0:T(8,128)S(1)} %dynamic-slice_bitcast_fusion.2, f32[8,16,8,256]{3,2,1,0:T(8,128)} %get-tuple-element.95), kind=kOutput, calls=%fused_computation.5.clone.1 | convolution fusion | flops 813694976 | bytes 1197056 | tf_op jit(solution)/shard_map/while/body/eval_jaxpr/ekt,etc->ekc/dot_general | solution.py:50
  62.8 0.7 dynamic-slice_bitcast_fusion.2
  63.5 12.3 %fusion.48 = f32[8,16,8,2048]{3,2,1,0:T(8,128)} fusion(f32[8,16,8,2048]{3,2,1,0:T(8,128)} %get-tuple-element.89, s32[]{:T(128)} %get-tuple-element.88, s32[16,256]{1,0:T(8,128)S(1)} %dynamic-slice_bitcast_fusion.2, f32[8,16,8,256]{3,2,1,0:T(8,128)} %get-tuple-element.95), kind=kOutput, calls=%fused_computation.5.clone.1 | convolution fusion | flops 813694976 | bytes 1197056 | tf_op jit(solution)/shard_map/while/body/eval_jaxpr/ekt,etc->ekc/dot_general | solution.py:50
  75.8 0.7 dynamic-slice_bitcast_fusion.2
  76.5 12.3 %fusion.48 = f32[8,16,8,2048]{3,2,1,0:T(8,128)} fusion(f32[8,16,8,2048]{3,2,1,0:T(8,128)} %get-tuple-element.89, s32[]{:T(128)} %get-tuple-element.88, s32[16,256]{1,0:T(8,128)S(1)} %dynamic-slice_bitcast_fusion.2, f32[8,16,8,256]{3,2,1,0:T(8,128)} %get-tuple-element.95), kind=kOutput, calls=%fused_computation.5.clone.1 | convolution fusion | flops 813694976 | bytes 1197056 | tf_op jit(solution)/shard_map/while/body/eval_jaxpr/ekt,etc->ekc/dot_general | solution.py:50
  88.9 0.7 dynamic-slice_bitcast_fusion.2
  89.6 12.3 %fusion.48 = f32[8,16,8,2048]{3,2,1,0:T(8,128)} fusion(f32[8,16,8,2048]{3,2,1,0:T(8,128)} %get-tuple-element.89, s32[]{:T(128)} %get-tuple-element.88, s32[16,256]{1,0:T(8,128)S(1)} %dynamic-slice_bitcast_fusion.2, f32[8,16,8,256]{3,2,1,0:T(8,128)} %get-tuple-element.95), kind=kOutput, calls=%fused_computation.5.clone.1 | convolution fusion | flops 813694976 | bytes 1197056 | tf_op jit(solution)/shard_map/while/body/eval_jaxpr/ekt,etc->ekc/dot_general | solution.py:50
  101.9 0.7 dynamic-slice_bitcast_fusion.2
  102.6 12.4 %fusion.48 = f32[8,16,8,2048]{3,2,1,0:T(8,128)} fusion(f32[8,16,8,2048]{3,2,1,0:T(8,128)} %get-tuple-element.89, s32[]{:T(128)} %get-tuple-element.88, s32[16,256]{1,0:T(8,128)S(1)} %dynamic-slice_bitcast_fusion.2, f32[8,16,8,256]{3,2,1,0:T(8,128)} %get-tuple-element.95), kind=kOutput, calls=%fused_computation.5.clone.1 | convolution fusion | flops 813694976 | bytes 1197056 | tf_op jit(solution)/shard_map/while/body/eval_jaxpr/ekt,etc->ekc/dot_general | solution.py:50
  115.0 0.0 copy-done.1
  115.0 9.1 %fusion.38 = f32[128,8,256]{2,1,0:T(8,128)S(1)} fusion(f32[128,8,2048]{2,1,0:T(8,128)} %bitcast.53, f32[2048,256,1]{1,0,2:T(8,128)S(1)} %bitcast.51), kind=kOutput, calls=%fused_computation.45 | convolution fusion | flops 6442450944 | bytes 11534336 | tf_op jit(solution)/shard_map/dot_general | solution.py:55
  124.1 0.0 copy-start.2
  124.1 1.6 fusion.23
  125.8 0.0 reduce-scatter.2.cloned.1.call-update
  125.8 0.0 all-gather.3.cloned.1.call-start
  125.8 0.5 all-gather.3.cloned.1.call-update
  126.4 0.0 all-gather.5.cloned.1.call-start
  126.4 0.0 copy-done.2
  126.4 1.5 fusion.37
  127.9 4.5 %collective-permute-start = (f32[1,32,32,256]{3,2,1,0:T(8,128)}, f32[1,32,32,256]{3,2,1,0:T(8,128)}, u32[]{:S(2)}, u32[]{:S(2)}) collective-permute-start(f32[1,32,32,256]{3,2,1,0:T(8,128)} %get-tuple-element.56), channel_id=1, source_target_pairs={{1,0},{2,1},{3,2},{4,3},{5,4},{6,5},{7,6},{0,7},{9,8},{10,9},{11,1... | collective-permute-start | bytes 3145736 | tf_op jit(solution)/shard_map/ppermute | solution.py:16
  132.4 0.0 collective-permute-start.1
  132.4 0.0 copy-start.5
  132.4 9.5 %copy.22 = f32[2048,1024]{1,0:T(8,128)} copy(f32[2048,1024]{0,1:T(8,128)} %bitcast.54) | data formatting | bytes 16777216 | tf_op jit(solution)/shard_map/rc,rb->cb/dot_general | solution.py:80
  142.0 0.0 copy-done.5
  142.0 0.1 fusion.34
  142.1 2.4 fusion.33
  144.5 0.0 copy-start.4
  144.5 2.5 fusion.35
  147.0 14.9 %reduce-scatter.2.cloned.1.call-done = f32[8,8,256]{2,0,1:T(8,128)} async-done(((f32[64,8,256]{2,0,1:T(8,128)}), f32[8,8,256]{2,0,1:T(8,128)}) %reduce-scatter.2.cloned.1.call-update) | async-done | bytes 65552 | tf_op jit(solution)/shard_map/reduce_scatter | solution.py:65
  161.9 0.0 copy-done.4
  161.9 0.0 copy-start.3
  161.9 1.2 convolution_bitcast_fusion
  163.1 15.2 %all_gather.10 = f32[64,8,256]{2,1,0:T(8,128)S(1)} all-gather(f32[8,8,256]{2,1,0:T(8,128)S(1)} %convolution_bitcast_fusion), channel_id=1, replica_groups=mesh['band'=4,'dom'=8] {'dom'}, dimensions={0}, use_global_device_ids=true | all-gather | bytes 589824 | tf_op jit(solution)/shard_map/all_gather | solution.py:76
  178.3 0.7 fusion.25
  179.0 0.0 collective-permute-done
  179.0 0.0 collective-permute-done.1
  179.1 0.0 copy-done.3
  179.1 13.1 %fusion.16 = f32[2,32,32,256]{3,2,1,0:T(8,128)} fusion(f32[2,32,32,256]{3,2,1,0:T(8,128)S(1)} %copy-done.2, f32[1,32,32,256]{3,2,1,0:T(8,128)} %collective-permute-done.1, f32[1,32,32,256]{3,2,1,0:T(8,128)} %collective-permute-done, f32[2,31,32,256]{3,2,1,0:T(8,128)} %get-tuple-element.53, f32[2,1,32,256]{3,2,1,0:T(8,128)S(1)} %get-tuple-element.55, ...), kind=kOutput, calls=%fused_computation.18 | convolution fusion | flops 6450315264 | bytes 24125440 | tf_op jit(solution)/shard_map/rc,rb->cb/dot_general | solution.py:80
  192.2 0.0 all-gather.5.cloned.1.call-update
  192.2 25.9 %all-gather.3.cloned.1.call-done = f32[2,32,32,1024]{3,2,1,0:T(8,128)} async-done(((f32[2,32,32,256]{3,2,1,0:T(8,128)}), f32[2,32,32,1024]{3,2,1,0:T(8,128)}) %all-gather.3.cloned.1.call-update) | async-done | bytes 8388624 | tf_op jit(solution)/shard_map/all_gather | solution.py:86
  218.1 0.0 copy-done
  218.1 10.0 %fusion.20 = f32[2,32,32,256]{3,2,1,0:T(8,128)} fusion(f32[2,32,32,1024]{3,2,1,0:T(8,128)} %all-gather.3.cloned.1.call-done, f32[1024,256]{1,0:T(8,128)S(1)} %copy-done), kind=kOutput, calls=%fused_computation.24 | convolution fusion | flops 6442450944 | bytes 11534336 | tf_op jit(solution)/shard_map/xyzb,bc->xyzc/dot_general | solution.py:84
  228.1 79.7 %all-gather.5.cloned.1.call-done = f32[2,32,32,1024]{3,2,1,0:T(8,128)} async-done(((f32[2,32,32,256]{3,2,1,0:T(8,128)}), f32[2,32,32,1024]{3,2,1,0:T(8,128)}) %all-gather.5.cloned.1.call-update) | async-done | bytes 8388624 | tf_op jit(solution)/shard_map/all_gather | solution.py:92
  307.8 10.0 %fusion.18 = f32[2,32,32,256]{3,2,1,0:T(8,128)} fusion(f32[2,32,32,1024]{3,2,1,0:T(8,128)} %all-gather.5.cloned.1.call-done, f32[1024,256]{1,0:T(8,128)S(1)} %copy-done), kind=kOutput, calls=%fused_computation.22 | convolution fusion | flops 6442450944 | bytes 11534336 | tf_op jit(solution)/shard_map/xyzb,bc->xyzc/dot_general | solution.py:90
  (3 shorter events, 0.0 us)
Async XLA Ops:
  8.0 210.1 %copy-start = (f32[1024,256]{1,0:T(8,128)S(1)}, f32[1024,256]{1,0:T(8,128)}, u32[]{:S(2)}) copy-start(f32[1024,256]{1,0:T(8,128)} %param.17) | copy-start | bytes 3145732
  8.0 153.9 %reduce-scatter.2.cloned.1.call-start = ((), (), s32[]{:S(2)}) async-start(), calls=%async_computation.2 | async-start | bytes 589824 | tf_op jit(solution)/shard_map/reduce_scatter | solution.py:65
  10.4 104.6 %copy-start.1 = (f32[2,32,32,256]{3,2,1,0:T(8,128)S(1)}, f32[2,32,32,256]{3,2,1,0:T(8,128)}, u32[]{:S(2)}) copy-start(f32[2,32,32,256]{3,2,1,0:T(8,128)} %param.10) | copy-start | bytes 6291460
  124.1 2.3 copy-start.2
  125.8 92.3 %all-gather.3.cloned.1.call-start = ((), (), s32[]{:S(2)}) async-start(), calls=%async_computation.1 | async-start | bytes 10485760 | tf_op jit(solution)/shard_map/all_gather | solution.py:86
  126.4 181.5 %all-gather.5.cloned.1.call-start = ((), (), s32[]{:S(2)}) async-start(), calls=%async_computation.3 | async-start | bytes 10485760 | tf_op jit(solution)/shard_map/all_gather | solution.py:92
  127.9 51.1 %collective-permute-start = (f32[1,32,32,256]{3,2,1,0:T(8,128)}, f32[1,32,32,256]{3,2,1,0:T(8,128)}, u32[]{:S(2)}, u32[]{:S(2)}) collective-permute-start(f32[1,32,32,256]{3,2,1,0:T(8,128)} %get-tuple-element.56), channel_id=1, source_target_pairs={{1,0},{2,1},{3,2},{4,3},{5,4},{6,5},{7,6},{0,7},{9,8},{10,9},{11,1... | collective-permute-start | bytes 3145736 | tf_op jit(solution)/shard_map/ppermute | solution.py:16
  132.4 46.6 %collective-permute-start.1 = (f32[1,32,32,256]{3,2,1,0:T(8,128)}, f32[1,32,32,256]{3,2,1,0:T(8,128)}, u32[]{:S(2)}, u32[]{:S(2)}) collective-permute-start(f32[1,32,32,256]{3,2,1,0:T(8,128)} %get-tuple-element.57), channel_id=1, source_target_pairs={{0,1},{1,2},{2,3},{3,4},{4,5},{5,6},{6,7},{7,0},{8,9},{9,10},{10,1... | collective-permute-start | bytes 3145736 | tf_op jit(solution)/shard_map/ppermute | solution.py:14
  132.4 9.5 %copy-start.5 = (f32[2,32,32]{2,1,0:T(8,128)S(1)}, f32[2,32,32]{2,1,0:T(8,128)}, u32[]{:S(2)}) copy-start(f32[2,32,32]{2,1,0:T(8,128)} %param.11) | copy-start | bytes 24580
  144.5 17.4 %copy-start.4 = (f32[8,8,8]{2,1,0:T(8,128)S(1)}, f32[8,8,8]{2,1,0:T(8,128)}, u32[]{:S(2)}) copy-start(f32[8,8,8]{2,1,0:T(8,128)} %param.16) | copy-start | bytes 6148
  161.9 17.1 %copy-start.3 = (f32[2,32,31,256]{3,2,1,0:T(8,128)S(1)}, f32[2,32,31,256]{3,2,1,0:T(8,128)}, u32[]{:S(2)}) copy-start(f32[2,32,31,256]{3,2,1,0:T(8,128)} %get-tuple-element.48) | copy-start | bytes 6094852
Sparse Core Ops, SparseCore 0:
  125.9 35.9 reduce-scatter.1
Sparse Core Ops, SparseCore 1:
  128.1 90.0 all-gather.2
  220.5 87.3 all-gather.4
where the time goes:
time: 326 us; the launch traced here: 325 us
  matrix products  144 us (44%)
  waiting for transfers between devices  121 us (37%)
  local copies, waits for them, and re-layouts  22.8 us (7%)
  between operations  15.6 us (5%)
  blocking collectives  15.2 us (5%)
  starting transfers between devices  4.61 us (1%)
    dot_general x8, matrix products, densify(): jnp.einsum('ekt,etc->ekc', values, one_hot, precision=lax.Precision.HIGHEST)  98.7 us
    all_gather x1, waiting for transfers between devices, body(): lax.all_gather(applied, 'band', axis=3, tiled=True)  79.7 us
    all_gather x1, waiting for transfers between devices, body(): lax.all_gather(orbitals, 'band', axis=3, tiled=True)  25.9 us
    all_gather x1, blocking collectives, body(): lax.all_gather(scaled, 'dom', axis=0, tiled=True)  15.2 us
    reduce_scatter x1, waiting for transfers between devices, body(): lax.psum_scatter(jnp.einsum('ea,ekb->akb', columns, partials, precision=l...  14.9 us
    dot_general x1, matrix products, body(): jnp.einsum('rc,rb->cb', dense_proj, returned_rows, precision=lax.Precisio...  13.1 us
    dot_general x1, matrix products, body(): jnp.einsum('xyzb,bc->xyzc', lax.all_gather(applied, 'band', axis=3, tiled...  10 us
    dot_general x1, matrix products, body(): jnp.einsum('xyzb,bc->xyzc', lax.all_gather(orbitals, 'band', axis=3, tile...  10 us
  transfers between devices with their start and end apart: 5, of which 3 were waited for; matrix products, arithmetic and copies ran while one was open for 13% of the time, Pallas kernels for 0%

commit v1 on v0

v1 whole, which is shorter than its diff:
```python
import functools

import jax
import jax.numpy as jnp
from jax import lax
from jax.experimental import pallas as pl
from jax.experimental.pallas import tpu as pltpu
from jax.sharding import PartitionSpec as P

LANES = 128
SUB = 8


def split(x):
    high = x.astype(jnp.bfloat16)
    low = (x - high.astype(jnp.float32)).astype(jnp.bfloat16)
    return high, low


def split_outside(x):
    high = lax.reduce_precision(x, exponent_bits=8, mantissa_bits=7)
    return high.astype(jnp.bfloat16), (x - high).astype(jnp.bfloat16)


def dot3(a, b, dims=(((1,), (0,)), ((), ()))):
    a_high, a_low = a
    b_high, b_low = b
    dot = functools.partial(lax.dot_general, dimension_numbers=dims, preferred_element_type=jnp.float32)
    return dot(a_high, b_high) + (dot(a_high, b_low) + dot(a_low, b_high))


def owner_rows(atom_ids, atom_owner):
    match = atom_ids[..., None] == jnp.arange(atom_owner.shape[0], dtype=jnp.int32)
    found_rows = jnp.sum(jnp.where(match, atom_owner, 0), axis=-1)
    return jnp.where(atom_ids >= 0, found_rows, -1)


def project_kernel(cells_ref, values_ref, high_ref, low_ref, dense_high, dense_low, partials_ref):
    tiles, proj, tile = values_ref.shape
    groups = dense_high.shape[1] // LANES
    lane_ids = lax.broadcasted_iota(jnp.int32, (LANES, tile), 0)

    def step(e, carry):
        cells = cells_ref[pl.ds(e, 1), :]
        group = jnp.broadcast_to(cells // LANES, (proj, tile))
        spot = jnp.broadcast_to(cells % LANES, (LANES, tile))
        hot = jnp.where(spot == lane_ids, 1.0, 0.0).astype(jnp.bfloat16)
        values = values_ref[e]
        high = values.astype(jnp.bfloat16).astype(jnp.float32)
        low = values - high
        rows = [jnp.where(group == g, high, 0.0) for g in range(groups)]
        rows += [jnp.where(group == g, low, 0.0) for g in range(groups)]
        left = jnp.concatenate(rows, axis=0).astype(jnp.bfloat16)
        out = lax.dot_general(
            left, hot, (((1,), (1,)), ((), ())), preferred_element_type=jnp.float32
        )
        half = groups * proj
        total = out[:half] + out[half:]
        row = jnp.concatenate([total[g * proj : (g + 1) * proj] for g in range(groups)], axis=1)
        return row

    def pair(i, carry):
        both = jnp.concatenate([step(2 * i, None), step(2 * i + 1, None)], axis=0)
        high, low = split(both)
        at = pl.ds(pl.multiple_of(i * 2 * proj, 2 * proj), 2 * proj)
        dense_high[at, :] = high
        dense_low[at, :] = low
        return carry

    lax.fori_loop(0, tiles // 2, pair, 0)
    partials_ref[...] = dot3(
        (dense_high[...], dense_low[...]), (high_ref[...], low_ref[...])
    )


def project(tile_cells, projectors, field_high, field_low):
    entries, proj, tile = projectors.shape
    cell_count, bands = field_high.shape
    block = 16
    rows = block * proj
    flops = 2 * entries * (2 * proj * cell_count * tile + 3 * proj * cell_count * bands)
    return pl.pallas_call(
        project_kernel,
        grid=(entries // block,),
        in_specs=[
            pl.BlockSpec((block, tile), lambda i: (i, 0)),
            pl.BlockSpec((block, proj, tile), lambda i: (i, 0, 0)),
            pl.BlockSpec((cell_count, bands), lambda i: (0, 0)),
            pl.BlockSpec((cell_count, bands), lambda i: (0, 0)),
        ],
        out_specs=[
            pl.BlockSpec((rows, cell_count), lambda i: (i, 0)),
            pl.BlockSpec((rows, cell_count), lambda i: (i, 0)),
            pl.BlockSpec((rows, bands), lambda i: (i, 0)),
        ],
        out_shape=[
            jax.ShapeDtypeStruct((entries * proj, cell_count), jnp.bfloat16),
            jax.ShapeDtypeStruct((entries * proj, cell_count), jnp.bfloat16),
            jax.ShapeDtypeStruct((entries * proj, bands), jnp.float32),
        ],
        compiler_params=pltpu.CompilerParams(vmem_limit_bytes=32 * 2**20),
        cost_estimate=pl.CostEstimate(flops=8 * flops, bytes_accessed=2**24, transcendentals=0),
        name="project",
    )(tile_cells, projectors, field_high, field_low)


def spread_kernel(dense_high, dense_low, back_high, back_low, far_ref):
    dims = (((0,), (0,)), ((), ()))
    far_ref[...] = dot3(
        (dense_high[...], dense_low[...]), (back_high[...], back_low[...]), dims
    )


def spread(dense_high, dense_low, back):
    rows, cell_count = dense_high.shape
    bands = back.shape[1]
    block = 256
    back_high, back_low = split_outside(back)
    return pl.pallas_call(
        spread_kernel,
        grid=(cell_count // block,),
        in_specs=[
            pl.BlockSpec((rows, block), lambda i: (0, i)),
            pl.BlockSpec((rows, block), lambda i: (0, i)),
            pl.BlockSpec((rows, bands), lambda i: (0, 0)),
            pl.BlockSpec((rows, bands), lambda i: (0, 0)),
        ],
        out_specs=pl.BlockSpec((block, bands), lambda i: (i, 0)),
        out_shape=jax.ShapeDtypeStruct((cell_count, bands), jnp.float32),
        compiler_params=pltpu.CompilerParams(vmem_limit_bytes=32 * 2**20),
        cost_estimate=pl.CostEstimate(
            flops=6 * rows * cell_count * bands, bytes_accessed=2**24, transcendentals=0
        ),
        name="spread",
    )(dense_high, dense_low, back_high, back_low)


def rotate_kernel(count, *refs):
    blocks, mats, out_ref = refs[:count], refs[count:-1], refs[-1]
    total = None
    for block, mat in zip(blocks, mats):
        term = dot3(split(block[...]), split(mat[...]))
        total = term if total is None else total + term
    out_ref[...] = total


def rotate(blocks, mats):
    rows, depth = blocks[0].shape
    bands = mats[0].shape[1]
    block = 256
    return pl.pallas_call(
        functools.partial(rotate_kernel, len(blocks)),
        grid=(rows // block,),
        in_specs=[pl.BlockSpec((block, depth), lambda i: (i, 0))] * len(blocks)
        + [pl.BlockSpec((depth, bands), lambda i: (0, 0))] * len(mats),
        out_specs=pl.BlockSpec((block, bands), lambda i: (i, 0)),
        out_shape=jax.ShapeDtypeStruct((rows, bands), jnp.float32),
        compiler_params=pltpu.CompilerParams(vmem_limit_bytes=32 * 2**20),
        cost_estimate=pl.CostEstimate(
            flops=6 * rows * depth * len(blocks) * bands, bytes_accessed=2**22, transcendentals=0
        ),
        name="rotate",
    )(*blocks, *mats)


def local_kernel(field_ref, before_ref, after_ref, weight_ref, far_ref, out_ref):
    planes = field_ref.shape[0]
    for p in range(planes):
        here = field_ref[p]
        low = before_ref[...] if p == 0 else field_ref[p - 1]
        high = after_ref[...] if p == planes - 1 else field_ref[p + 1]
        beside = low + high
        beside = beside + jnp.roll(here, 1, 0) + jnp.roll(here, -1, 0)
        beside = beside + jnp.roll(here, 1, 1) + jnp.roll(here, -1, 1)
        out_ref[p] = weight_ref[p] * here - 0.5 * beside + far_ref[p]


def local_apply(field, before, after, weight, far):
    planes, ny, nz, bands = field.shape
    whole = pl.BlockSpec((planes, ny, nz, LANES), lambda i: (0, 0, 0, i))
    side = pl.BlockSpec((ny, nz, LANES), lambda i: (0, 0, i))
    return pl.pallas_call(
        local_kernel,
        grid=(bands // LANES,),
        in_specs=[
            whole,
            side,
            side,
            pl.BlockSpec((planes, ny, nz, LANES), lambda i: (0, 0, 0, 0)),
            whole,
        ],
        out_specs=whole,
        out_shape=jax.ShapeDtypeStruct(field.shape, jnp.float32),
        compiler_params=pltpu.CompilerParams(vmem_limit_bytes=40 * 2**20),
        cost_estimate=pl.CostEstimate(
            flops=12 * planes * ny * nz * bands, bytes_accessed=2**23, transcendentals=0
        ),
        name="local",
    )(field, before, after, weight, far)


def gather_blocks(field, parts):
    count = lax.axis_size("band")
    me = lax.axis_index("band")
    rows = field.shape[0] // parts
    pieces = [field[i * rows : (i + 1) * rows] for i in range(parts)]
    if count != 4:
        out = []
        for piece in pieces:
            whole = lax.all_gather(piece, "band", axis=0)
            out.append([whole[i] for i in range(count)])
        return out, list(range(count))
    flip = lambda k: [(i, i ^ k) for i in range(count)]
    out = []
    for piece in pieces:
        one = lax.ppermute(piece, "band", flip(1))
        two = lax.ppermute(piece, "band", flip(2))
        half = rows // 2
        three = jnp.concatenate(
            [
                lax.ppermute(one[:half], "band", flip(2)),
                lax.ppermute(two[half:], "band", flip(1)),
            ],
            axis=0,
        )
        out.append([piece, one, two, three])
    return out, [me ^ k for k in range(count)]


def body(orbitals, potential, projectors, tile_cells, tile_atom, atom_owner, coupling, rotation):
    planes, ny, nz, bands = orbitals.shape
    cell_count = planes * ny * nz
    entries, proj, _ = projectors.shape
    atom_total = atom_owner.shape[0]
    dom_count = lax.axis_size("dom")
    domain_index = lax.axis_index("dom")
    field = orbitals.reshape(cell_count, bands)
    blocks, owners = gather_blocks(field, planes)
    mats = [lax.dynamic_slice_in_dim(rotation, o * bands, bands, axis=0) for o in owners]

    field_high, field_low = split_outside(field)
    dense_high, dense_low, partials = project(tile_cells, projectors, field_high, field_low)
    my_atoms = lax.dynamic_slice_in_dim(tile_atom, domain_index * entries, entries)
    my_rows = owner_rows(my_atoms, atom_owner)
    columns = (my_rows[:, None] == jnp.arange(atom_total, dtype=jnp.int32)[None, :]).astype(
        jnp.float32
    )
    sums = jnp.einsum(
        "ea,ekb->akb",
        columns,
        partials.reshape(entries, proj, bands),
        precision=lax.Precision.HIGHEST,
    )
    owned = lax.psum_scatter(sums, "dom", scatter_dimension=0, tiled=True)
    scaled = jnp.einsum("akj,ajb->akb", coupling, owned, precision=lax.Precision.HIGHEST)
    scaled = scaled.reshape(-1, bands)
    scaled = lax.all_gather(scaled, "band", axis=1, tiled=True)
    scaled = jnp.dot(scaled, rotation, precision=lax.Precision.HIGHEST)
    scaled = lax.all_gather(scaled, "dom", axis=0, tiled=True).reshape(atom_total, proj, bands)
    back = jnp.einsum("ea,akb->ekb", columns, scaled, precision=lax.Precision.HIGHEST)
    far = spread(dense_high, dense_low, back.reshape(entries * proj, bands))

    weight = jnp.broadcast_to((3.0 + potential)[..., None], (planes, ny, nz, LANES))
    rotated = [rotate(part, mats).reshape(ny, nz, bands) for part in blocks]
    after = lax.ppermute(rotated[0], "dom", [((i + 1) % dom_count, i) for i in range(dom_count)])
    before = lax.ppermute(rotated[-1], "dom", [(i, (i + 1) % dom_count) for i in range(dom_count)])
    first = jnp.stack(rotated, axis=0)
    second = local_apply(first, before, after, weight, far.reshape(orbitals.shape))
    return first, second


def solution(mesh):
    return jax.shard_map(
        body,
        mesh=mesh,
        in_specs=(
            P("dom", None, None, "band"),
            P("dom", None, None),
            P("dom", None, None),
            P("dom", None),
            P(),
            P(),
            P("dom", None, None),
            P(None, "band"),
        ),
        out_specs=(P("dom", None, None, "band"), P("dom", None, None, "band")),
        check_vma=False,
    )
```

time: 326 us -> 149 us (0.46)
  matrix products: 144 us -> 4.49 us
  waiting for transfers between devices: 121 us -> 19.1 us
  Pallas kernels: 0 us -> 37 us
  blocking collectives: 15.2 us -> 36.5 us
  starting transfers between devices: 4.61 us -> 12.8 us
  local copies, waits for them, and re-layouts: 22.8 us -> 18.4 us
  other arithmetic: 1.51 us -> 5.89 us
    dot_general x15 -> x4, matrix products: 144 us -> 4.49 us  [the longest x1 1.87 us: body(): scaled = jnp.dot(scaled, rotation, precision=lax.Precision.HIGHEST)]
    all_gather x2 -> x0, waiting for transfers between devices: 106 us -> none  [the longest x1 79.7 us: body(): lax.all_gather(applied, 'band', axis=3, tiled=True)]
    pallas_call x0 -> x5, Pallas kernels: none -> 37 us  [the longest x1 20.5 us: project(): pl.pallas_call(project_kernel, grid=(entries // block,), in_specs=[pl.Blo...]
    all_gather x1, blocking collectives: 15.2 us -> 27.5 us  [body(): lax.all_gather(scaled, 'dom', axis=0, tiled=True)]
    all_gather x0 -> x1, blocking collectives: none -> 8.98 us  [body(): scaled = lax.all_gather(scaled, 'band', axis=1, tiled=True)]
    dot_general x1, local copies, waits for them, and re-layouts: 9.54 us -> 1.12 us  [body(): jnp.einsum('ea,ekb->akb', columns, partials.reshape(entries, proj, bands)...]
    ppermute x2 -> x10, starting transfers between devices: 4.48 us -> 12.7 us  [the longest x2 4.06 us: gather_blocks(): lax.ppermute(one[:half], 'band', flip(2))]
    unnamed x12 -> x32, local copies, waits for them, and re-layouts: 0.03 us -> 7.7 us
  transfers between devices with their start and end apart: 5 -> 11, of which waited for: 3 -> 2; matrix products, arithmetic and copies ran while one was open for 13% -> 13% of each run, Pallas kernels for 0% -> 23%
where the time goes in v1:
time: 149 us; the launch traced here: 148 us
  Pallas kernels  37 us (25%)
  blocking collectives  36.5 us (24%)
  waiting for transfers between devices  19.1 us (13%)
  local copies, waits for them, and re-layouts  18.4 us (12%)
  between operations  14.3 us (10%)
  starting transfers between devices  12.8 us (9%)
  other arithmetic  5.89 us (4%)
  matrix products  4.49 us (3%)
    all_gather x1, blocking collectives, body(): lax.all_gather(scaled, 'dom', axis=0, tiled=True)  27.5 us
    pallas_call x1, Pallas kernels, project(): pl.pallas_call(project_kernel, grid=(entries // block,), in_specs=[pl.Blo...  20.5 us
    reduce_scatter x1, waiting for transfers between devices, body(): owned = lax.psum_scatter(sums, 'dom', scatter_dimension=0, tiled=True)  14.3 us
    all_gather x1, blocking collectives, body(): scaled = lax.all_gather(scaled, 'band', axis=1, tiled=True)  8.98 us
    pallas_call x2, Pallas kernels, rotate(): pl.pallas_call(functools.partial(rotate_kernel, len(blocks)), grid=(rows...  7.91 us
    unnamed x32, local copies, waits for them, and re-layouts  7.7 us
    pallas_call x1, Pallas kernels, spread(): pl.pallas_call(spread_kernel, grid=(cell_count // block,), in_specs=[pl.B...  6.24 us
    ppermute x2, waiting for transfers between devices, gather_blocks(): one = lax.ppermute(piece, 'band', flip(1))  4.74 us
  transfers between devices with their start and end apart: 11, of which 2 were waited for; matrix products, arithmetic and copies ran while one was open for 13% of the time, Pallas kernels for 23%

profile of v1, /device:TPU:0, one launch (start us, length us, event | category | flops | bytes accessed | tf_op | source)
XLA Modules:
  0.0 148.5 jit_solution(14390873765856685074)
XLA Ops:
  7.2 0.0 copy-start
  7.2 0.0 reduce-scatter.2.cloned.1.call-start
  7.2 0.0 copy-start.12
  7.2 1.9 %fusion.11 = (f32[1,32,32,256]{3,2,1,0:T(8,128)S(1)}, f32[1,32,32,256]{3,2,1,0:T(8,128)S(1)}) fusion(f32[2,32,32,256]{3,2,1,0:T(8,128)} %param.8), kind=kLoop, calls=%fused_computation.26 | loop fusion | bytes 4194304 | tf_op jit(solution)/shard_map/slice | solution.py:206
  9.2 3.0 %collective-permute-start = (f32[1024,256]{1,0:T(8,128)S(1)}, f32[1024,256]{1,0:T(8,128)S(1)}, u32[]{:S(2)}, u32[]{:S(2)}) collective-permute-start(f32[1024,256]{1,0:T(8,128)S(1)} %bitcast.30), channel_id=1, source_target_pairs={{0,8},{8,0},{16,24},{24,16},{1,9},{9,1},{17,25},{25,17},{2,10},{10... | collective-permute-start | bytes 3145736 | tf_op jit(solution)/shard_map/ppermute | solution.py:216
  12.2 1.5 %collective-permute-start.1 = (f32[1024,256]{1,0:T(8,128)S(1)}, f32[1024,256]{1,0:T(8,128)}, u32[]{:S(2)}, u32[]{:S(2)}) collective-permute-start(f32[1024,256]{1,0:T(8,128)S(1)} %bitcast.31), channel_id=1, source_target_pairs={{0,16},{8,24},{16,0},{24,8},{1,17},{9,25},{17,1},{25,9},{2,18},{10... | collective-permute-start | bytes 3145736 | tf_op jit(solution)/shard_map/ppermute | solution.py:217
  13.7 0.5 collective-permute-start.4
  14.2 0.1 collective-permute-start.5
  14.3 1.6 %fusion = (bf16[2048,256]{1,0:T(8,128)(2,1)}, bf16[2048,256]{1,0:T(8,128)(2,1)}) fusion(f32[2,32,32,256]{3,2,1,0:T(8,128)S(1)} %copy-done.12), kind=kLoop, calls=%fused_computation.2 | loop fusion | flops 2097152 | bytes 4194304 | tf_op jit(solution)/shard_map/convert_element_type | solution.py:22
  15.9 0.8 dynamic_slice.19
  16.7 0.1 select_reduce_fusion
  16.8 0.8 compare_select_fusion
  17.6 0.0 copy-done.7
  17.6 1.2 copy-done.4
  18.8 1.2 copy-done.5
  20.0 1.2 copy-done.6
  21.2 20.5 %project.1 = (bf16[1024,2048]{1,0:T(8,128)(2,1)S(1)}, bf16[1024,2048]{1,0:T(8,128)(2,1)S(1)}, f32[1024,256]{1,0:T(8,128)S(1)}) custom-call(s32[128,256]{1,0:T(8,128)S(1)} %copy-done.7, f32[128,8,256]{2,1,0:T(8,128)S(1)} %copy-done.6, bf16[2048,256]{1,0:T(8,128)(2,1)S(1)} %copy-done.5, bf16[2048,256]{1,0:T(8,128)(2,1)S(1)} %copy-done.4), custom_call_target="tpu_custom_call" | custom-call | flops 42949672960 | bytes 16777216 | tf_op jit(solution)/shard_map/project/pallas_call | solution.py:82
  41.7 1.9 %copy-done.8 = bf16[1024,2048]{1,0:T(8,128)(2,1)} copy-done((bf16[1024,2048]{1,0:T(8,128)(2,1)}, bf16[1024,2048]{1,0:T(8,128)(2,1)S(1)}, u32[]{:S(2)}) %copy-start.8) | copy-done | bytes 4194328
  43.7 2.0 %copy-done.10 = bf16[1024,2048]{1,0:T(8,128)(2,1)} copy-done((bf16[1024,2048]{1,0:T(8,128)(2,1)}, bf16[1024,2048]{1,0:T(8,128)(2,1)S(1)}, u32[]{:S(2)}) %copy-start.10) | copy-done | bytes 4194328
  45.7 0.8 fusion.2
  46.5 1.1 copy.15
  47.6 0.0 reduce-scatter.2.cloned.1.call-update
  47.7 0.0 copy-start.13
  47.7 0.0 collective-permute-done.refs_1_
  47.7 0.0 copy-start.2
  47.7 0.8 slice.32
  48.6 2.0 %collective-permute-start.2 = (f32[512,256]{1,0:T(8,128)}, f32[512,256]{1,0:T(8,128)}, u32[]{:S(2)}, u32[]{:S(2)}) collective-permute-start(f32[512,256]{1,0:T(8,128)} %slice.32), channel_id=1, source_target_pairs={{0,16},{8,24},{16,0},{24,8},{1,17},{9,25},{17,1},{25,9},{2,18},{10... | collective-permute-start | bytes 1572872 | tf_op jit(solution)/shard_map/ppermute | solution.py:221
  50.5 0.0 collective-permute-done.1.refs_2_
  50.5 1.9 %slice.33 = f32[512,256]{1,0:T(8,128)} slice(f32[1024,256]{1,0:T(8,128)} %collective-permute-done.1.refs_2_), slice={[512:1024], [0:256]} | slice | bytes 1048576 | tf_op jit(solution)/shard_map/slice | solution.py:222
  52.4 1.5 %collective-permute-start.3 = (f32[512,256]{1,0:T(8,128)}, f32[512,256]{1,0:T(8,128)}, u32[]{:S(2)}, u32[]{:S(2)}) collective-permute-start(f32[512,256]{1,0:T(8,128)} %slice.33), channel_id=1, source_target_pairs={{0,8},{8,0},{16,24},{24,16},{1,9},{9,1},{17,25},{25,17},{2,10},{10... | collective-permute-start | bytes 1572872 | tf_op jit(solution)/shard_map/ppermute | solution.py:222
  53.9 0.1 constant_dynamic-slice_fusion
  54.0 4.7 %collective-permute-done.4.refs_1_ = f32[1024,256]{1,0:T(8,128)} collective-permute-done((f32[1024,256]{1,0:T(8,128)S(1)}, f32[1024,256]{1,0:T(8,128)}, u32[]{:S(2)}, u32[]{:S(2)}) %collective-permute-start.4) | collective-permute-done | bytes 1048608 | tf_op jit(solution)/shard_map/ppermute | solution.py:216
  58.7 1.9 %slice.34 = f32[512,256]{1,0:T(8,128)} slice(f32[1024,256]{1,0:T(8,128)} %collective-permute-done.4.refs_1_), slice={[0:512], [0:256]} | slice | bytes 1048576 | tf_op jit(solution)/shard_map/slice | solution.py:221
  60.6 2.1 %collective-permute-start.6 = (f32[512,256]{1,0:T(8,128)}, f32[512,256]{1,0:T(8,128)}, u32[]{:S(2)}, u32[]{:S(2)}) collective-permute-start(f32[512,256]{1,0:T(8,128)} %slice.34), channel_id=1, source_target_pairs={{0,16},{8,24},{16,0},{24,8},{1,17},{9,25},{17,1},{25,9},{2,18},{10... | collective-permute-start | bytes 1572872 | tf_op jit(solution)/shard_map/ppermute | solution.py:221
  62.7 0.0 collective-permute-done.5.refs_2_
  62.7 1.9 %slice.35 = f32[512,256]{1,0:T(8,128)} slice(f32[1024,256]{1,0:T(8,128)} %collective-permute-done.5.refs_2_), slice={[512:1024], [0:256]} | slice | bytes 1048576 | tf_op jit(solution)/shard_map/slice | solution.py:222
  64.6 1.5 %collective-permute-start.7 = (f32[512,256]{1,0:T(8,128)}, f32[512,256]{1,0:T(8,128)}, u32[]{:S(2)}, u32[]{:S(2)}) collective-permute-start(f32[512,256]{1,0:T(8,128)} %slice.35), channel_id=1, source_target_pairs={{0,8},{8,0},{16,24},{24,16},{1,9},{9,1},{17,25},{25,17},{2,10},{10... | collective-permute-start | bytes 1572872 | tf_op jit(solution)/shard_map/ppermute | solution.py:222
  66.1 14.3 %reduce-scatter.2.cloned.1.call-done = f32[8,8,256]{2,1,0:T(8,128)} async-done(((f32[64,8,256]{2,1,0:T(8,128)}), f32[8,8,256]{2,1,0:T(8,128)}) %reduce-scatter.2.cloned.1.call-update) | async-done | bytes 65552 | tf_op jit(solution)/shard_map/reduce_scatter | solution.py:254
  80.4 1.1 convolution_bitcast_fusion
  81.5 9.0 %all_gather.6 = f32[64,1024]{1,0:T(8,128)S(1)} all-gather(f32[64,256]{1,0:T(8,128)S(1)} %convolution_bitcast_fusion), channel_id=1, replica_groups=mesh['band'=4,'dom'=8] {'band'}, dimensions={1}, use_global_device_ids=true | all-gather | bytes 327680 | tf_op jit(solution)/shard_map/all_gather | solution.py:257
  90.5 1.9 %fusion.12 = f32[64,256]{1,0:T(8,128)S(1)} fusion(f32[64,1024]{1,0:T(8,128)S(1)} %all_gather.6, f32[1024,256]{1,0:T(8,128)} %param.15), kind=kOutput, calls=%fused_computation.27 | convolution fusion | flops 201326592 | bytes 1376256 | tf_op jit(solution)/shard_map/dot_general | solution.py:258
  92.4 0.0 collective-permute-done.2
  92.4 0.0 collective-permute-done.3
  92.4 1.3 pad_maximum_fusion.1.refs_3_
  93.7 3.8 %rotate.2 = f32[1024,256]{1,0:T(8,128)S(1)} custom-call(f32[1024,256]{1,0:T(8,128)S(1)} %bitcast.32, f32[1024,256]{1,0:T(8,128)S(1)} %copy-done.3, f32[1024,256]{1,0:T(8,128)} %collective-permute-done.1.refs_2_, f32[1024,256]{1,0:T(8,128)S(1)} %pad_maximum_fusion.1.refs_3_, f32[256,256]{1,0:T(8,128)S(1)} %get-tuple-element.17.refs_4_, ...), custom_call_target="tpu_custom_call" | custom-call | flops 1610612736 | bytes 4194304 | tf_op jit(solution)/shard_map/rotate/pallas_call | solution.py:151
  97.5 0.1 collective-permute-start.9
  97.5 0.0 collective-permute-done.6
  97.5 0.0 collective-permute-done.7
  97.6 1.3 pad_maximum_fusion.2.refs_3_
  98.8 0.0 copy-start.11
  98.8 4.1 %rotate.3 = f32[1024,256]{1,0:T(8,128)S(1)} custom-call(f32[1024,256]{1,0:T(8,128)S(1)} %bitcast.29, f32[1024,256]{1,0:T(8,128)} %collective-permute-done.4.refs_1_, f32[1024,256]{1,0:T(8,128)} %collective-permute-done.5.refs_2_, f32[1024,256]{1,0:T(8,128)S(1)} %pad_maximum_fusion.2.refs_3_, f32[256,256]{1,0:T(8,128)S(1)} %get-tuple-element.17.refs_4_, ...), custom_call_target="tpu_custom_call" | custom-call | flops 1610612736 | bytes 4194304 | tf_op jit(solution)/shard_map/rotate/pallas_call | solution.py:151
  103.0 0.5 collective-permute-start.8
  103.5 27.5 %all_gather.7 = f32[512,256]{1,0:T(8,128)S(1)} all-gather(f32[64,256]{1,0:T(8,128)S(1)} %fusion.12), channel_id=1, replica_groups=mesh['band'=4,'dom'=8] {'dom'}, dimensions={0}, use_global_device_ids=true | all-gather | bytes 589824 | tf_op jit(solution)/shard_map/all_gather | solution.py:259
  131.1 0.7 fusion.4
  131.8 0.6 fusion.1
  132.4 0.0 copy-done.11
  132.4 0.0 copy-done.9
  132.4 6.2 %spread.1 = f32[2048,256]{1,0:T(8,128)S(1)} custom-call(bf16[1024,2048]{1,0:T(8,128)(2,1)S(1)} %copy-done.9, bf16[1024,2048]{1,0:T(8,128)(2,1)S(1)} %copy-done.11, bf16[1024,256]{1,0:T(8,128)(2,1)S(1)} %get-tuple-element.13.back_high, bf16[1024,256]{1,0:T(8,128)(2,1)S(1)} %get-tuple-element.12.back_low), custom_call_target="tpu_custom_call" | custom-call | flops 3221225472 | bytes 16777216 | tf_op jit(solution)/shard_map/spread/pallas_call | solution.py:119
  138.7 0.2 pad_maximum_fusion.field_ref
  138.9 0.0 copy-start.1
  138.9 0.0 collective-permute-done.9.after_ref
  138.9 0.0 collective-permute-done.8.before_ref
  138.9 0.3 broadcast_in_dim.22.weight_ref
  139.3 2.3 %local.1 = f32[2,32,32,256]{3,2,1,0:T(8,128)} custom-call(f32[2,32,32,256]{3,2,1,0:T(8,128)S(1)} %pad_maximum_fusion.field_ref, f32[32,32,256]{2,1,0:T(8,128)S(1)} %collective-permute-done.8.before_ref, f32[32,32,256]{2,1,0:T(8,128)S(1)} %collective-permute-done.9.after_ref, f32[2,32,32,128]{3,2,1,0:T(8,128)S(1)} %broadcast_in_dim.22.weight_ref, ...), custom_call_target="tpu_custom_call" | custom-call | flops 6291456 | bytes 8388608 | tf_op jit(solution)/shard_map/local/pallas_call | solution.py:182
  (19 shorter events, 0.0 us)
Async XLA Ops:
  7.2 73.2 %copy-start = (f32[8,8,8]{2,1,0:T(8,128)S(1)}, f32[8,8,8]{2,1,0:T(8,128)}, u32[]{:S(2)}) copy-start(f32[8,8,8]{2,1,0:T(8,128)} %param.14) | copy-start | bytes 6148
  7.2 73.2 %reduce-scatter.2.cloned.1.call-start = ((), (), s32[]{:S(2)}) async-start(), calls=%async_computation.1 | async-start | bytes 589824 | tf_op jit(solution)/shard_map/reduce_scatter | solution.py:254
  7.2 7.1 %copy-start.12 = (f32[2,32,32,256]{3,2,1,0:T(8,128)S(1)}, f32[2,32,32,256]{3,2,1,0:T(8,128)}, u32[]{:S(2)}) copy-start(f32[2,32,32,256]{3,2,1,0:T(8,128)} %param.8) | copy-start | bytes 6291460
  9.2 38.5 %collective-permute-start = (f32[1024,256]{1,0:T(8,128)S(1)}, f32[1024,256]{1,0:T(8,128)S(1)}, u32[]{:S(2)}, u32[]{:S(2)}) collective-permute-start(f32[1024,256]{1,0:T(8,128)S(1)} %bitcast.30), channel_id=1, source_target_pairs={{0,8},{8,0},{16,24},{24,16},{1,9},{9,1},{17,25},{25,17},{2,10},{10... | collective-permute-start | bytes 3145736 | tf_op jit(solution)/shard_map/ppermute | solution.py:216
  12.2 38.4 %collective-permute-start.1 = (f32[1024,256]{1,0:T(8,128)S(1)}, f32[1024,256]{1,0:T(8,128)}, u32[]{:S(2)}, u32[]{:S(2)}) collective-permute-start(f32[1024,256]{1,0:T(8,128)S(1)} %bitcast.31), channel_id=1, source_target_pairs={{0,16},{8,24},{16,0},{24,8},{1,17},{9,25},{17,1},{25,9},{2,18},{10... | collective-permute-start | bytes 3145736 | tf_op jit(solution)/shard_map/ppermute | solution.py:217
  13.7 45.0 %collective-permute-start.4 = (f32[1024,256]{1,0:T(8,128)S(1)}, f32[1024,256]{1,0:T(8,128)}, u32[]{:S(2)}, u32[]{:S(2)}) collective-permute-start(f32[1024,256]{1,0:T(8,128)S(1)} %bitcast.27), channel_id=1, source_target_pairs={{0,8},{8,0},{16,24},{24,16},{1,9},{9,1},{17,25},{25,17},{2,10},{10... | collective-permute-start | bytes 3145736 | tf_op jit(solution)/shard_map/ppermute | solution.py:216
  14.2 48.5 %collective-permute-start.5 = (f32[1024,256]{1,0:T(8,128)S(1)}, f32[1024,256]{1,0:T(8,128)}, u32[]{:S(2)}, u32[]{:S(2)}) collective-permute-start(f32[1024,256]{1,0:T(8,128)S(1)} %bitcast.28), channel_id=1, source_target_pairs={{0,16},{8,24},{16,0},{24,8},{1,17},{9,25},{17,1},{25,9},{2,18},{10... | collective-permute-start | bytes 3145736 | tf_op jit(solution)/shard_map/ppermute | solution.py:217
  14.3 2.4 %copy-start.15 = (s32[64]{0:T(128)S(1)}, s32[64]{0:T(128)}, u32[]{:S(2)}) copy-start(s32[64]{0:T(128)} %param.13) | copy-start | bytes 772
  14.3 3.3 %copy-start.7 = (s32[128,256]{1,0:T(8,128)S(1)}, s32[128,256]{1,0:T(8,128)}, u32[]{:S(2)}) copy-start(s32[128,256]{1,0:T(8,128)} %cells_ref.1) | copy-start | bytes 393220
  17.6 1.2 copy-start.4
  18.8 1.2 copy-start.5
  20.0 1.2 copy-start.6
  41.7 1.9 %copy-start.8 = (bf16[1024,2048]{1,0:T(8,128)(2,1)}, bf16[1024,2048]{1,0:T(8,128)(2,1)S(1)}, u32[]{:S(2)}) copy-start(bf16[1024,2048]{1,0:T(8,128)(2,1)S(1)} %get-tuple-element.5.dense_high) | copy-start | bytes 12582916
  43.7 2.0 %copy-start.10 = (bf16[1024,2048]{1,0:T(8,128)(2,1)}, bf16[1024,2048]{1,0:T(8,128)(2,1)S(1)}, u32[]{:S(2)}) copy-start(bf16[1024,2048]{1,0:T(8,128)(2,1)S(1)} %get-tuple-element.6.dense_low) | copy-start | bytes 12582916
  45.7 2.0 %copy-start.14 = (f32[2,32,32]{2,1,0:T(8,128)S(1)}, f32[2,32,32]{2,1,0:T(8,128)}, u32[]{:S(2)}) copy-start(f32[2,32,32]{2,1,0:T(8,128)} %param.9) | copy-start | bytes 24580
  47.7 6.2 %copy-start.13 = (f32[1024,256]{1,0:T(8,128)S(1)}, f32[1024,256]{1,0:T(8,128)}, u32[]{:S(2)}) copy-start(f32[1024,256]{1,0:T(8,128)} %param.15) | copy-start | bytes 3145732
  47.7 4.7 %copy-start.2 = (f32[1024,256]{1,0:T(8,128)}, f32[1024,256]{1,0:T(8,128)S(1)}, u32[]{:S(2)}) copy-start(f32[1024,256]{1,0:T(8,128)S(1)} %collective-permute-done.refs_1_) | copy-start | bytes 3145732
  48.6 43.8 %collective-permute-start.2 = (f32[512,256]{1,0:T(8,128)}, f32[512,256]{1,0:T(8,128)}, u32[]{:S(2)}, u32[]{:S(2)}) collective-permute-start(f32[512,256]{1,0:T(8,128)} %slice.32), channel_id=1, source_target_pairs={{0,16},{8,24},{16,0},{24,8},{1,17},{9,25},{17,1},{25,9},{2,18},{10... | collective-permute-start | bytes 1572872 | tf_op jit(solution)/shard_map/ppermute | solution.py:221
  52.4 40.0 %collective-permute-start.3 = (f32[512,256]{1,0:T(8,128)}, f32[512,256]{1,0:T(8,128)}, u32[]{:S(2)}, u32[]{:S(2)}) collective-permute-start(f32[512,256]{1,0:T(8,128)} %slice.33), channel_id=1, source_target_pairs={{0,8},{8,0},{16,24},{24,16},{1,9},{9,1},{17,25},{25,17},{2,10},{10... | collective-permute-start | bytes 1572872 | tf_op jit(solution)/shard_map/ppermute | solution.py:222
  60.6 36.9 %collective-permute-start.6 = (f32[512,256]{1,0:T(8,128)}, f32[512,256]{1,0:T(8,128)}, u32[]{:S(2)}, u32[]{:S(2)}) collective-permute-start(f32[512,256]{1,0:T(8,128)} %slice.34), channel_id=1, source_target_pairs={{0,16},{8,24},{16,0},{24,8},{1,17},{9,25},{17,1},{25,9},{2,18},{10... | collective-permute-start | bytes 1572872 | tf_op jit(solution)/shard_map/ppermute | solution.py:221
  64.6 33.0 %collective-permute-start.7 = (f32[512,256]{1,0:T(8,128)}, f32[512,256]{1,0:T(8,128)}, u32[]{:S(2)}, u32[]{:S(2)}) collective-permute-start(f32[512,256]{1,0:T(8,128)} %slice.35), channel_id=1, source_target_pairs={{0,8},{8,0},{16,24},{24,16},{1,9},{9,1},{17,25},{25,17},{2,10},{10... | collective-permute-start | bytes 1572872 | tf_op jit(solution)/shard_map/ppermute | solution.py:222
  80.4 13.3 %copy-start.3 = (f32[1024,256]{1,0:T(8,128)S(1)}, f32[1024,256]{1,0:T(8,128)}, u32[]{:S(2)}) copy-start(f32[1024,256]{1,0:T(8,128)} %copy-done.2) | copy-start | bytes 3145732
  97.5 41.5 %collective-permute-start.9 = (f32[32,32,256]{2,1,0:T(8,128)S(1)}, f32[32,32,256]{2,1,0:T(8,128)S(1)}, u32[]{:S(2)}, u32[]{:S(2)}) collective-permute-start(f32[32,32,256]{2,1,0:T(8,128)S(1)} %bitcast.33), channel_id=1, source_target_pairs={{1,0},{2,1},{3,2},{4,3},{5,4},{6,5},{7,6},{0,7},{9,8},{10,9},{11,1... | collective-permute-start | bytes 3145736 | tf_op jit(solution)/shard_map/ppermute | solution.py:265
  98.8 33.6 %copy-start.11 = (bf16[1024,2048]{1,0:T(8,128)(2,1)S(1)}, bf16[1024,2048]{1,0:T(8,128)(2,1)}, u32[]{:S(2)}) copy-start(bf16[1024,2048]{1,0:T(8,128)(2,1)} %copy-done.10) | copy-start | bytes 12582916
  103.0 29.4 %copy-start.9 = (bf16[1024,2048]{1,0:T(8,128)(2,1)S(1)}, bf16[1024,2048]{1,0:T(8,128)(2,1)}, u32[]{:S(2)}) copy-start(bf16[1024,2048]{1,0:T(8,128)(2,1)} %copy-done.8) | copy-start | bytes 12582916
  103.0 36.0 %collective-permute-start.8 = (f32[32,32,256]{2,1,0:T(8,128)S(1)}, f32[32,32,256]{2,1,0:T(8,128)S(1)}, u32[]{:S(2)}, u32[]{:S(2)}) collective-permute-start(f32[32,32,256]{2,1,0:T(8,128)S(1)} %bitcast.35), channel_id=1, source_target_pairs={{0,1},{1,2},{2,3},{3,4},{4,5},{5,6},{6,7},{7,0},{8,9},{9,10},{10,1... | collective-permute-start | bytes 3145736 | tf_op jit(solution)/shard_map/ppermute | solution.py:266
  138.9 2.7 %copy-start.1 = (f32[2,32,32,256]{3,2,1,0:T(8,128)}, f32[2,32,32,256]{3,2,1,0:T(8,128)S(1)}, u32[]{:S(2)}) copy-start(f32[2,32,32,256]{3,2,1,0:T(8,128)S(1)} %pad_maximum_fusion.field_ref) | copy-start | bytes 6291460
Sparse Core Ops, SparseCore 0:
  47.8 32.6 reduce-scatter.1

commit v2 on v1

--- a/solution.py
+++ b/solution.py
@@ -35,7 +35,13 @@
     return jnp.where(atom_ids >= 0, found_rows, -1)
 
 
-def project_kernel(cells_ref, values_ref, high_ref, low_ref, dense_high, dense_low, partials_ref):
+def project_kernel(
+    cells_ref, values_ref, field_ref, dense_high, dense_low, partials_ref, high_ref, low_ref
+):
+    @pl.when(pl.program_id(0) == 0)
+    def _():
+        high_ref[...], low_ref[...] = split(field_ref[...])
+
     tiles, proj, tile = values_ref.shape
     groups = dense_high.shape[1] // LANES
     lane_ids = lax.broadcasted_iota(jnp.int32, (LANES, tile), 0)
@@ -73,9 +79,9 @@
     )
 
 
-def project(tile_cells, projectors, field_high, field_low):
+def project(tile_cells, projectors, field):
     entries, proj, tile = projectors.shape
-    cell_count, bands = field_high.shape
+    cell_count, bands = field.shape
     block = 16
     rows = block * proj
     flops = 2 * entries * (2 * proj * cell_count * tile + 3 * proj * cell_count * bands)
@@ -85,7 +91,6 @@
         in_specs=[
             pl.BlockSpec((block, tile), lambda i: (i, 0)),
             pl.BlockSpec((block, proj, tile), lambda i: (i, 0, 0)),
-            pl.BlockSpec((cell_count, bands), lambda i: (0, 0)),
             pl.BlockSpec((cell_count, bands), lambda i: (0, 0)),
         ],
         out_specs=[
@@ -98,10 +103,140 @@
             jax.ShapeDtypeStruct((entries * proj, cell_count), jnp.bfloat16),
             jax.ShapeDtypeStruct((entries * proj, bands), jnp.float32),
         ],
+        scratch_shapes=[pltpu.VMEM((cell_count, bands), jnp.bfloat16)] * 2,
         compiler_params=pltpu.CompilerParams(vmem_limit_bytes=32 * 2**20),
         cost_estimate=pl.CostEstimate(flops=8 * flops, bytes_accessed=2**24, transcendentals=0),
         name="project",
-    )(tile_cells, projectors, field_high, field_low)
+    )(tile_cells, projectors, field)
+
+
+def exchange_kernel(
+    sums_ref, coupling_ref, mats_ref, out_ref, arrived, mine, others,
+    send_sums, recv_sums, send_mine, recv_mine, send_out, recv_out,
+):
+    dom_count, band_count = sums_ref.shape[0], mats_ref.shape[0]
+    dom, band = lax.axis_index("dom"), lax.axis_index("band")
+    mesh_id = pl.DeviceIdType.MESH
+    barrier = pltpu.get_barrier_semaphore()
+
+    def dom_peer(k):
+        return lax.rem(dom + k, dom_count)
+
+    def band_peer(k):
+        return lax.rem(band + k, band_count)
+
+    def greet(k, carry):
+        pl.semaphore_signal(barrier, inc=1, device_id={"dom": dom_peer(k)}, device_id_type=mesh_id)
+        return carry
+
+    lax.fori_loop(1, dom_count, greet, 0)
+    for k in range(1, band_count):
+        pl.semaphore_signal(barrier, inc=1, device_id={"band": band_peer(k)}, device_id_type=mesh_id)
+    pl.semaphore_wait(barrier, dom_count - 1 + band_count - 1)
+
+    def sums_copy(k):
+        return pltpu.make_async_remote_copy(
+            src_ref=sums_ref.at[dom_peer(k)],
+            dst_ref=arrived.at[k],
+            send_sem=send_sums.at[k],
+            recv_sem=recv_sums.at[k],
+            device_id={"dom": dom_peer(k)},
+            device_id_type=mesh_id,
+        )
+
+    def mine_copy(k):
+        return pltpu.make_async_remote_copy(
+            src_ref=mine,
+            dst_ref=others.at[k],
+            send_sem=send_mine.at[k],
+            recv_sem=recv_mine.at[k],
+            device_id={"band": band_peer(k)},
+            device_id_type=mesh_id,
+        )
+
+    def out_copy(k):
+        return pltpu.make_async_remote_copy(
+            src_ref=out_ref.at[dom],
+            dst_ref=out_ref.at[dom],
+            send_sem=send_out.at[k],
+            recv_sem=recv_out.at[k],
+            device_id={"dom": dom_peer(k)},
+            device_id_type=mesh_id,
+        )
+
+    def start(copy):
+        def step(k, carry):
+            copy(k).start()
+            return carry
+
+        return step
+
+    def add(k, total):
+        sums_copy(k).wait_recv()
+        return total + arrived[k]
+
+    lax.fori_loop(1, dom_count, start(sums_copy), 0)
+    total = lax.fori_loop(1, dom_count, add, sums_ref[dom])
+    mine[...] = dot3(split(coupling_ref[...]), split(total))
+    for k in range(1, band_count):
+        mine_copy(k).start()
+    result = dot3(split(mine[...]), split(mats_ref[band]))
+    for k in range(1, band_count):
+        mine_copy(k).wait_recv()
+        source = lax.rem(band - k + band_count, band_count)
+        result = result + dot3(split(others[k]), split(mats_ref[source]))
+    out_ref[dom] = result
+    lax.fori_loop(1, dom_count, start(out_copy), 0)
+
+    def finish(k, carry):
+        source = lax.rem(dom - k + dom_count, dom_count)
+        pltpu.make_async_remote_copy(
+            src_ref=out_ref.at[dom],
+            dst_ref=out_ref.at[source],
+            send_sem=send_out.at[k],
+            recv_sem=recv_out.at[k],
+            device_id={"dom": dom_peer(k)},
+            device_id_type=mesh_id,
+        ).wait()
+        sums_copy(k).wait_send()
+        return carry
+
+    lax.fori_loop(1, dom_count, finish, 0)
+    for k in range(1, band_count):
+        mine_copy(k).wait_send()
+
+
+def exchange(sums, coupling, mats):
+    dom_count, rows, bands = sums.shape
+    band_count = mats.shape[0]
+    vmem = pl.BlockSpec(memory_space=pltpu.VMEM)
+    dma = pltpu.SemaphoreType.DMA
+    return pl.pallas_call(
+        exchange_kernel,
+        in_specs=[vmem] * 3,
+        out_specs=vmem,
+        out_shape=jax.ShapeDtypeStruct(sums.shape, jnp.float32),
+        scratch_shapes=[
+            pltpu.VMEM(sums.shape, jnp.float32),
+            pltpu.VMEM((rows, bands), jnp.float32),
+            pltpu.VMEM((band_count, rows, bands), jnp.float32),
+            dma((dom_count,)),
+            dma((dom_count,)),
+            dma((band_count,)),
+            dma((band_count,)),
+            dma((dom_count,)),
+            dma((dom_count,)),
+        ],
+        compiler_params=pltpu.CompilerParams(
+            vmem_limit_bytes=32 * 2**20, collective_id=0, has_side_effects=True
+        ),
+        cost_estimate=pl.CostEstimate(
+            flops=6 * rows * band_count * bands * bands,
+            bytes_accessed=2**24,
+            transcendentals=0,
+        ),
+        name="exchange",
+    )(sums, coupling, mats)
 
 
 def spread_kernel(dense_high, dense_low, back_high, back_low, far_ref):
@@ -163,40 +298,43 @@
     )(*blocks, *mats)
 
 
-def local_kernel(field_ref, before_ref, after_ref, weight_ref, far_ref, out_ref):
-    planes = field_ref.shape[0]
+def local_kernel(count, sides, *refs):
+    items, refs = refs[:count], refs[count:]
+    before, refs = refs[:sides], refs[sides:]
+    after, refs = refs[:sides], refs[sides:]
+    weight_ref, far_ref, first_ref, second_ref = refs
+    planes, ny = first_ref.shape[:2]
+    step = ny // sides
+    for i, item in enumerate(items):
+        at = (i % sides) * step
+        first_ref[i // sides, at : at + step] = item[...]
     for p in range(planes):
-        here = field_ref[p]
-        low = before_ref[...] if p == 0 else field_ref[p - 1]
-        high = after_ref[...] if p == planes - 1 else field_ref[p + 1]
+        here = first_ref[p]
+        low = jnp.concatenate([r[...] for r in before], 0) if p == 0 else first_ref[p - 1]
+        high = jnp.concatenate([r[...] for r in after], 0) if p == planes - 1 else first_ref[p + 1]
         beside = low + high
         beside = beside + jnp.roll(here, 1, 0) + jnp.roll(here, -1, 0)
         beside = beside + jnp.roll(here, 1, 1) + jnp.roll(here, -1, 1)
-        out_ref[p] = weight_ref[p] * here - 0.5 * beside + far_ref[p]
-
-
-def local_apply(field, before, after, weight, far):
-    planes, ny, nz, bands = field.shape
+        second_ref[p] = weight_ref[p] * here - 0.5 * beside + far_ref[p]
+
+
+def local_apply(items, before, after, weight, far):
+    planes, ny, nz, bands = far.shape
     whole = pl.BlockSpec((planes, ny, nz, LANES), lambda i: (0, 0, 0, i))
-    side = pl.BlockSpec((ny, nz, LANES), lambda i: (0, 0, i))
+    part = pl.BlockSpec((items[0].shape[0], nz, LANES), lambda i: (0, 0, i))
     return pl.pallas_call(
-        local_kernel,
+        functools.partial(local_kernel, len(items), len(before)),
         grid=(bands // LANES,),
-        in_specs=[
-            whole,
-            side,
-            side,
-            pl.BlockSpec((planes, ny, nz, LANES), lambda i: (0, 0, 0, 0)),
-            whole,
-        ],
-        out_specs=whole,
-        out_shape=jax.ShapeDtypeStruct(field.shape, jnp.float32),
+        in_specs=[part] * (len(items) + 2 * len(before))
+        + [pl.BlockSpec((planes, ny, nz, LANES), lambda i: (0, 0, 0, 0)), whole],
+        out_specs=[whole, whole],
+        out_shape=[jax.ShapeDtypeStruct(far.shape, jnp.float32)] * 2,
         compiler_params=pltpu.CompilerParams(vmem_limit_bytes=40 * 2**20),
         cost_estimate=pl.CostEstimate(
             flops=12 * planes * ny * nz * bands, bytes_accessed=2**23, transcendentals=0
         ),
         name="local",
-    )(field, before, after, weight, far)
+    )(*items, *before, *after, weight, far)
 
 
 def gather_blocks(field, parts):
@@ -211,18 +349,13 @@
             out.append([whole[i] for i in range(count)])
         return out, list(range(count))
     flip = lambda k: [(i, i ^ k) for i in range(count)]
+    direct = [
+        (piece, lax.ppermute(piece, "band", flip(1)), lax.ppermute(piece, "band", flip(2)))
+        for piece in pieces
+    ]
     out = []
-    for piece in pieces:
-        one = lax.ppermute(piece, "band", flip(1))
-        two = lax.ppermute(piece, "band", flip(2))
-        half = rows // 2
-        three = jnp.concatenate(
-            [
-                lax.ppermute(one[:half], "band", flip(2)),
-                lax.ppermute(two[half:], "band", flip(1)),
-            ],
-            axis=0,
-        )
+    for i, (piece, one, two) in enumerate(direct):
+        three = lax.ppermute(one, "band", flip(2)) if i % 2 == 0 else lax.ppermute(two, "band", flip(1))
         out.append([piece, one, two, three])
     return out, [me ^ k for k in range(count)]
 
@@ -235,11 +368,11 @@
     dom_count = lax.axis_size("dom")
     domain_index = lax.axis_index("dom")
     field = orbitals.reshape(cell_count, bands)
-    blocks, owners = gather_blocks(field, planes)
-    mats = [lax.dynamic_slice_in_dim(rotation, o * bands, bands, axis=0) for o in owners]
-
-    field_high, field_low = split_outside(field)
-    dense_high, dense_low, partials = project(tile_cells, projectors, field_high, field_low)
+    sides = 2
+    blocks, owners = gather_blocks(field, planes * sides)
+    band_mats = rotation.reshape(-1, bands, bands)
+    mats = [lax.dynamic_index_in_dim(band_mats, o, axis=0, keepdims=False) for o in owners]
+    dense_high, dense_low, partials = project(tile_cells, projectors, field)
     my_atoms = lax.dynamic_slice_in_dim(tile_atom, domain_index * entries, entries)
     my_rows = owner_rows(my_atoms, atom_owner)
     columns = (my_rows[:, None] == jnp.arange(atom_total, dtype=jnp.int32)[None, :]).astype(
@@ -251,21 +384,21 @@
         partials.reshape(entries, proj, bands),
         precision=lax.Precision.HIGHEST,
     )
-    owned = lax.psum_scatter(sums, "dom", scatter_dimension=0, tiled=True)
-    scaled = jnp.einsum("akj,ajb->akb", coupling, owned, precision=lax.Precision.HIGHEST)
-    scaled = scaled.reshape(-1, bands)
-    scaled = lax.all_gather(scaled, "band", axis=1, tiled=True)
-    scaled = jnp.dot(scaled, rotation, precision=lax.Precision.HIGHEST)
-    scaled = lax.all_gather(scaled, "dom", axis=0, tiled=True).reshape(atom_total, proj, bands)
+    own = coupling.shape[0]
+    eye = jnp.eye(own, dtype=bool)[:, None, :, None]
+    coupled = jnp.where(eye, coupling[:, :, None, :], 0.0).reshape(own * proj, own * proj)
+    scaled = exchange(sums.reshape(dom_count, own * proj, bands), coupled, band_mats)
+    scaled = scaled.reshape(atom_total, proj, bands)
     back = jnp.einsum("ea,akb->ekb", columns, scaled, precision=lax.Precision.HIGHEST)
     far = spread(dense_high, dense_low, back.reshape(entries * proj, bands))
 
     weight = jnp.broadcast_to((3.0 + potential)[..., None], (planes, ny, nz, LANES))
-    rotated = [rotate(part, mats).reshape(ny, nz, bands) for part in blocks]
-    after = lax.ppermute(rotated[0], "dom", [((i + 1) % dom_count, i) for i in range(dom_count)])
-    before = lax.ppermute(rotated[-1], "dom", [(i, (i + 1) % dom_count) for i in range(dom_count)])
-    first = jnp.stack(rotated, axis=0)
-    second = local_apply(first, before, after, weight, far.reshape(orbitals.shape))
+    rotated = [rotate(part, mats).reshape(-1, nz, bands) for part in blocks]
+    down = [((i + 1) % dom_count, i) for i in range(dom_count)]
+    up = [(i, (i + 1) % dom_count) for i in range(dom_count)]
+    after = [lax.ppermute(item, "dom", down) for item in rotated[:sides]]
+    before = [lax.ppermute(item, "dom", up) for item in rotated[-sides:]]
+    first, second = local_apply(rotated, before, after, weight, far.reshape(orbitals.shape))
     return first, second
 
 

time: 149 us -> 128 us (0.86)
  blocking collectives: 36.5 us -> 0 us
  Pallas kernels: 37 us -> 73.1 us
  between operations: 14.3 us -> 0.86 us
  starting transfers between devices: 12.8 us -> 22.3 us
  local copies, waits for them, and re-layouts: 18.4 us -> 9.75 us
  other arithmetic: 5.89 us -> 1.63 us
  matrix products: 4.49 us -> 2.48 us
  waiting for transfers between devices: 19.1 us -> 17.4 us
    all_gather x2 -> x0, blocking collectives: 36.5 us -> none  [the longest x1 27.5 us: body(): lax.all_gather(scaled, 'dom', axis=0, tiled=True)]
    pallas_call x1 -> x2, Pallas kernels: 2.33 us -> 37.5 us  [the longest x1 33.8 us: exchange(): pl.pallas_call(exchange_kernel, in_specs=[vmem] * 3, out_specs=vmem, out_...]
    reduce_scatter x1 -> x0, waiting for transfers between devices: 14.3 us -> none  [body(): owned = lax.psum_scatter(sums, 'dom', scatter_dimension=0, tiled=True)]
    ppermute x10 -> x16, waiting for transfers between devices: 4.76 us -> 17.4 us  [the longest x2 9.75 us: gather_blocks(): lax.ppermute(one, 'band', flip(2))]
    ppermute x10 -> x16, starting transfers between devices: 12.7 us -> 22.3 us  [the longest x4 5.68 us: gather_blocks(): lax.ppermute(piece, 'band', flip(1))]
    slice x4 -> x0, local copies, waits for them, and re-layouts: 6.48 us -> none  [the longest x2 3.74 us: gather_blocks(): two[half:]]
    dot_general x2 -> x0, matrix products: 2.98 us -> none  [the longest x1 1.87 us: body(): scaled = jnp.dot(scaled, rotation, precision=lax.Precision.HIGHEST)]
    concatenate x2 -> x0, other arithmetic: 2.54 us -> none  [gather_blocks(): jnp.concatenate([lax.ppermute(one[:half], 'band', flip(2)), lax.ppermute(...]
  transfers between devices with their start and end apart: 11 -> 16, of which waited for: 2 -> 4; matrix products, arithmetic and copies ran while one was open for 13% -> 4% of each run, Pallas kernels for 23% -> 54%
where the time goes in v2:
time: 128 us
  Pallas kernels  73.1 us (57%)
  starting transfers between devices  22.3 us (17%)
  waiting for transfers between devices  17.4 us (14%)
  local copies, waits for them, and re-layouts  9.75 us (8%)
  matrix products  2.48 us (2%)
  other arithmetic  1.63 us (1%)
    pallas_call x1, Pallas kernels, exchange(): pl.pallas_call(exchange_kernel, in_specs=[vmem] * 3, out_specs=vmem, out_...  33.8 us
    pallas_call x1, Pallas kernels, project(): pl.pallas_call(project_kernel, grid=(entries // block,), in_specs=[pl.Blo...  20.8 us
    ppermute x2, waiting for transfers between devices, gather_blocks(): lax.ppermute(one, 'band', flip(2))  9.75 us
    pallas_call x4, Pallas kernels, rotate(): pl.pallas_call(functools.partial(rotate_kernel, len(blocks)), grid=(rows...  8.57 us
    ppermute x2, waiting for transfers between devices, gather_blocks(): lax.ppermute(two, 'band', flip(1))  7.25 us
    pallas_call x1, Pallas kernels, spread(): pl.pallas_call(spread_kernel, grid=(cell_count // block,), in_specs=[pl.B...  6.24 us
    ppermute x4, starting transfers between devices, gather_blocks(): lax.ppermute(piece, 'band', flip(1))  5.68 us
    ppermute x4, starting transfers between devices, gather_blocks(): lax.ppermute(piece, 'band', flip(2))  5.61 us
  transfers between devices with their start and end apart: 16, of which 4 were waited for; matrix products, arithmetic and copies ran while one was open for 4% of the time, Pallas kernels for 54%

profile of v2, /device:TPU:0, one launch (start us, length us, event | category | flops | bytes accessed | tf_op | source)
XLA Modules:
  0.0 127.5 jit_solution(15293249739633243872)
XLA Ops:
  0.6 0.0 copy-start.1
  0.6 0.0 copy-start.3
  0.6 2.9 %fusion.10 = (f32[512,256]{1,0:T(8,128)}, f32[512,256]{1,0:T(8,128)}, f32[512,256]{1,0:T(8,128)S(1)}, f32[512,256]{1,0:T(8,128)S(1)}) fusion(f32[2048,256]{1,0:T(8,128)} %bitcast.38), kind=kLoop, calls=%fused_computation.21 | loop fusion | bytes 4194304 | tf_op jit(solution)/shard_map/slice | solution.py:344
  3.6 3.0 %collective-permute-start.10 = (f32[512,256]{1,0:T(8,128)}, f32[512,256]{1,0:T(8,128)}, u32[]{:S(2)}, u32[]{:S(2)}) collective-permute-start(f32[512,256]{1,0:T(8,128)} %get-tuple-element.8.refs_0_), channel_id=1, source_target_pairs={{0,16},{8,24},{16,0},{24,8},{1,17},{9,25},{17,1},{25,9},{2,18},{10... | collective-permute-start | bytes 1572872 | tf_op jit(solution)/shard_map/ppermute | solution.py:353
  6.5 1.5 %collective-permute-start.9 = (f32[512,256]{1,0:T(8,128)}, f32[512,256]{1,0:T(8,128)}, u32[]{:S(2)}, u32[]{:S(2)}) collective-permute-start(f32[512,256]{1,0:T(8,128)} %get-tuple-element.8.refs_0_), channel_id=1, source_target_pairs={{0,8},{8,0},{16,24},{24,16},{1,9},{9,1},{17,25},{25,17},{2,10},{10... | collective-permute-start | bytes 1572872 | tf_op jit(solution)/shard_map/ppermute | solution.py:353
  8.0 0.5 collective-permute-start.6
  8.5 0.0 collective-permute-start.7
  8.6 2.0 %collective-permute-start.4 = (f32[512,256]{1,0:T(8,128)S(1)}, f32[512,256]{1,0:T(8,128)}, u32[]{:S(2)}, u32[]{:S(2)}) collective-permute-start(f32[512,256]{1,0:T(8,128)S(1)} %get-tuple-element.10.refs_0_), channel_id=1, source_target_pairs={{0,16},{8,24},{16,0},{24,8},{1,17},{9,25},{17,1},{25,9},{2,18},{10... | collective-permute-start | bytes 1572872 | tf_op jit(solution)/shard_map/ppermute | solution.py:353
  10.6 0.8 dynamic_slice.20
  11.3 0.0 copy-done.1
  11.3 0.0 copy-done.3
  11.3 1.2 copy-done.2
  12.6 20.8 %project.1 = (bf16[1024,2048]{1,0:T(8,128)(2,1)S(1)}, bf16[1024,2048]{1,0:T(8,128)(2,1)S(1)}, f32[1024,256]{1,0:T(8,128)S(1)}) custom-call(s32[128,256]{1,0:T(8,128)S(1)} %copy-done.3, f32[128,8,256]{2,1,0:T(8,128)S(1)} %copy-done.2, f32[2048,256]{1,0:T(8,128)S(1)} %bitcast.39), custom_call_target="tpu_custom_call" | custom-call | flops 42949672960 | bytes 16777216 | tf_op jit(solution)/shard_map/project/pallas_call | solution.py:88
  33.3 0.0 copy-start.4
  33.4 1.9 %copy-done.4 = bf16[1024,2048]{1,0:T(8,128)(2,1)} copy-done((bf16[1024,2048]{1,0:T(8,128)(2,1)}, bf16[1024,2048]{1,0:T(8,128)(2,1)S(1)}, u32[]{:S(2)}) %copy-start.4) | copy-done | bytes 4194328
  35.3 2.0 %copy-done.6 = bf16[1024,2048]{1,0:T(8,128)(2,1)} copy-done((bf16[1024,2048]{1,0:T(8,128)(2,1)}, bf16[1024,2048]{1,0:T(8,128)(2,1)S(1)}, u32[]{:S(2)}) %copy-start.6) | copy-done | bytes 4194328
  37.3 0.0 copy-done.11
  37.3 0.1 select_reduce_fusion
  37.4 0.8 compare_select_fusion
  38.3 0.8 fusion.1
  39.1 0.0 collective-permute-done.10.refs_2_
  39.1 1.6 %collective-permute-start = (f32[512,256]{1,0:T(8,128)S(1)}, f32[512,256]{1,0:T(8,128)S(1)}, u32[]{:S(2)}, u32[]{:S(2)}) collective-permute-start(f32[512,256]{1,0:T(8,128)S(1)} %get-tuple-element.11.refs_0_), channel_id=1, source_target_pairs={{0,8},{8,0},{16,24},{24,16},{1,9},{9,1},{17,25},{25,17},{2,10},{10... | collective-permute-start | bytes 1572872 | tf_op jit(solution)/shard_map/ppermute | solution.py:353
  40.7 0.0 collective-permute-done.9.refs_1_
  40.7 0.5 collective-permute-start.11
  41.2 0.3 copy.15
  41.5 0.0 copy-done.9
  41.5 0.1 broadcast_select_fusion
  41.6 0.1 select_n.40.coupling_ref
  41.7 33.8 %exchange.1 = f32[8,64,256]{2,1,0:T(8,128)S(1)} custom-call(f32[8,64,256]{2,1,0:T(8,128)S(1)} %bitcast.41, f32[64,64]{1,0:T(8,128)S(1)} %select_n.40.coupling_ref, f32[4,256,256]{2,1,0:T(8,128)S(1)} %bitcast.27), custom_call_target="tpu_custom_call" | custom-call | flops 100663296 | bytes 16777216 | tf_op jit(solution)/shard_map/exchange/pallas_call | solution.py:214
  75.5 0.0 collective-permute-done.6.refs_1_
  75.5 0.4 collective-permute-start.8
  75.9 1.7 %fusion.3 = f32[128,8,256]{2,0,1:T(8,128)} fusion(f32[64,8,256]{2,1,0:T(8,128)S(1)} %bitcast.40, s32[128]{0:T(128)S(1)} %compare_select_fusion), kind=kOutput, calls=%fused_computation.5 | convolution fusion | flops 201334784 | bytes 1573376 | tf_op jit(solution)/shard_map/ea,akb->ekb/dot_general | solution.py:392
  77.6 0.0 collective-permute-done.7.refs_2_
  77.6 2.0 %collective-permute-start.3 = (f32[512,256]{1,0:T(8,128)S(1)}, f32[512,256]{1,0:T(8,128)S(1)}, u32[]{:S(2)}, u32[]{:S(2)}) collective-permute-start(f32[512,256]{1,0:T(8,128)S(1)} %get-tuple-element.10.refs_0_), channel_id=1, source_target_pairs={{0,8},{8,0},{16,24},{24,16},{1,9},{9,1},{17,25},{25,17},{2,10},{10... | collective-permute-start | bytes 1572872 | tf_op jit(solution)/shard_map/ppermute | solution.py:353
  79.7 0.0 collective-permute-done.4.refs_2_
  79.7 0.6 collective-permute-start.1
  80.3 0.0 collective-permute-done.refs_1_
  80.3 1.1 collective-permute-start.5
  81.4 0.0 collective-permute-done.11.refs_3_
  81.4 0.4 collective-permute-start.2
  81.8 0.1 dynamic-slice_bitcast_fusion
  81.9 0.6 fusion
  82.5 2.5 %rotate.7 = f32[512,256]{1,0:T(8,128)S(1)} custom-call(f32[512,256]{1,0:T(8,128)} %get-tuple-element.8.refs_0_, f32[512,256]{1,0:T(8,128)} %collective-permute-done.9.refs_1_, f32[512,256]{1,0:T(8,128)} %collective-permute-done.10.refs_2_, f32[512,256]{1,0:T(8,128)} %collective-permute-done.11.refs_3_, f32[256,256]{1,0:T(8,128)S(1)} %get-tuple-element.17.refs_4_, ...), custom_call_target="tpu_custom_call" | custom-call | flops 805306368 | bytes 4194304 | tf_op jit(solution)/shard_map/rotate/pallas_call | solution.py:286
  85.0 5.3 %collective-permute-done.8.refs_3_ = f32[512,256]{1,0:T(8,128)S(1)} collective-permute-done((f32[512,256]{1,0:T(8,128)}, f32[512,256]{1,0:T(8,128)S(1)}, u32[]{:S(2)}, u32[]{:S(2)}) %collective-permute-start.8) | collective-permute-done | bytes 524320 | tf_op jit(solution)/shard_map/ppermute | solution.py:358
  90.4 0.6 collective-permute-start.13
  91.0 2.5 %rotate.6 = f32[512,256]{1,0:T(8,128)S(1)} custom-call(f32[512,256]{1,0:T(8,128)} %get-tuple-element.9.refs_0_, f32[512,256]{1,0:T(8,128)} %collective-permute-done.6.refs_1_, f32[512,256]{1,0:T(8,128)} %collective-permute-done.7.refs_2_, f32[512,256]{1,0:T(8,128)S(1)} %collective-permute-done.8.refs_3_, f32[256,256]{1,0:T(8,128)S(1)} %get-tuple-element.17.refs_4_, ...), custom_call_target="tpu_custom_call" | custom-call | flops 805306368 | bytes 4194304 | tf_op jit(solution)/shard_map/rotate/pallas_call | solution.py:286
  93.5 0.0 collective-permute-done.3.refs_1_
  93.5 2.7 %collective-permute-start.12 = (f32[16,32,256]{2,1,0:T(8,128)S(1)}, f32[16,32,256]{2,1,0:T(8,128)S(1)}, u32[]{:S(2)}, u32[]{:S(2)}) collective-permute-start(f32[16,32,256]{2,1,0:T(8,128)S(1)} %bitcast.31), channel_id=1, source_target_pairs={{0,1},{1,2},{2,3},{3,4},{4,5},{5,6},{6,7},{7,0},{8,9},{9,10},{10,1... | collective-permute-start | bytes 1572872 | tf_op jit(solution)/shard_map/ppermute | solution.py:400
  96.2 7.3 %collective-permute-done.5.refs_3_ = f32[512,256]{1,0:T(8,128)S(1)} collective-permute-done((f32[512,256]{1,0:T(8,128)}, f32[512,256]{1,0:T(8,128)S(1)}, u32[]{:S(2)}, u32[]{:S(2)}) %collective-permute-start.5) | collective-permute-done | bytes 524320 | tf_op jit(solution)/shard_map/ppermute | solution.py:358
  103.4 2.3 %rotate.5 = f32[512,256]{1,0:T(8,128)S(1)} custom-call(f32[512,256]{1,0:T(8,128)S(1)} %get-tuple-element.10.refs_0_, f32[512,256]{1,0:T(8,128)S(1)} %collective-permute-done.3.refs_1_, f32[512,256]{1,0:T(8,128)} %collective-permute-done.4.refs_2_, f32[512,256]{1,0:T(8,128)S(1)} %collective-permute-done.5.refs_3_, f32[256,256]{1,0:T(8,128)S(1)} %get-tuple-element.17.refs_4_, ...), custom_call_target="tpu_custom_call" | custom-call | flops 805306368 | bytes 4194304 | tf_op jit(solution)/shard_map/rotate/pallas_call | solution.py:286
  105.8 0.0 copy-start.10
  105.8 2.6 %collective-permute-start.15 = (f32[16,32,256]{2,1,0:T(8,128)S(1)}, f32[16,32,256]{2,1,0:T(8,128)S(1)}, u32[]{:S(2)}, u32[]{:S(2)}) collective-permute-start(f32[16,32,256]{2,1,0:T(8,128)S(1)} %bitcast.33), channel_id=1, source_target_pairs={{1,0},{2,1},{3,2},{4,3},{5,4},{6,5},{7,6},{0,7},{9,8},{10,9},{11,1... | collective-permute-start | bytes 1572872 | tf_op jit(solution)/shard_map/ppermute | solution.py:399
  108.4 0.0 collective-permute-done.1.refs_2_
  108.4 4.4 %collective-permute-done.2.refs_3_ = f32[512,256]{1,0:T(8,128)S(1)} collective-permute-done((f32[512,256]{1,0:T(8,128)S(1)}, f32[512,256]{1,0:T(8,128)S(1)}, u32[]{:S(2)}, u32[]{:S(2)}) %collective-permute-start.2) | collective-permute-done | bytes 524320 | tf_op jit(solution)/shard_map/ppermute | solution.py:358
  112.8 1.2 rotate.4
  114.1 2.7 %collective-permute-start.14 = (f32[16,32,256]{2,1,0:T(8,128)S(1)}, f32[16,32,256]{2,1,0:T(8,128)S(1)}, u32[]{:S(2)}, u32[]{:S(2)}) collective-permute-start(f32[16,32,256]{2,1,0:T(8,128)S(1)} %bitcast.35), channel_id=1, source_target_pairs={{1,0},{2,1},{3,2},{4,3},{5,4},{6,5},{7,6},{0,7},{9,8},{10,9},{11,1... | collective-permute-start | bytes 1572872 | tf_op jit(solution)/shard_map/ppermute | solution.py:399
  116.7 0.0 copy-done.10
  116.8 6.2 %spread.1 = f32[2048,256]{1,0:T(8,128)S(1)} custom-call(bf16[1024,2048]{1,0:T(8,128)(2,1)S(1)} %copy-done.5, bf16[1024,2048]{1,0:T(8,128)(2,1)S(1)} %copy-done.7, bf16[1024,256]{1,0:T(8,128)(2,1)S(1)} %get-tuple-element.13.back_high, bf16[1024,256]{1,0:T(8,128)(2,1)S(1)} %get-tuple-element.12.back_low), custom_call_target="tpu_custom_call" | custom-call | flops 3221225472 | bytes 16777216 | tf_op jit(solution)/shard_map/spread/pallas_call | solution.py:254
  123.0 0.0 collective-permute-done.13.refs_5_
  123.0 0.0 collective-permute-done.12.refs_4_
  123.0 0.0 collective-permute-done.15.refs_7_
  123.1 0.4 collective-permute-done.14.refs_6_
  123.4 0.3 broadcast_in_dim.44.refs_8_
  123.8 3.7 %local.1 = (f32[2,32,32,256]{3,2,1,0:T(8,128)}, f32[2,32,32,256]{3,2,1,0:T(8,128)}) custom-call(f32[16,32,256]{2,1,0:T(8,128)S(1)} %bitcast.36, f32[16,32,256]{2,1,0:T(8,128)S(1)} %bitcast.34, f32[16,32,256]{2,1,0:T(8,128)S(1)} %bitcast.32, f32[16,32,256]{2,1,0:T(8,128)S(1)} %bitcast.30, f32[16,32,256]{2,1,0:T(8,128)S(1)} %collective-permute-done.12.refs_4_, ...), custom_call_target="tpu_custom_call" | custom-call | flops 6291456 | bytes 8388608 | tf_op jit(solution)/shard_map/local/pallas_call | solution.py:325
  (14 shorter events, 0.0 us)
Async XLA Ops:
  0.6 10.7 %copy-start.1 = (f32[2,32,32,256]{3,2,1,0:T(8,128)S(1)}, f32[2,32,32,256]{3,2,1,0:T(8,128)}, u32[]{:S(2)}) copy-start(f32[2,32,32,256]{3,2,1,0:T(8,128)} %param.8) | copy-start | bytes 6291460
  0.6 10.7 %copy-start.3 = (s32[128,256]{1,0:T(8,128)S(1)}, s32[128,256]{1,0:T(8,128)}, u32[]{:S(2)}) copy-start(s32[128,256]{1,0:T(8,128)} %cells_ref.1) | copy-start | bytes 393220
  3.6 35.5 %collective-permute-start.10 = (f32[512,256]{1,0:T(8,128)}, f32[512,256]{1,0:T(8,128)}, u32[]{:S(2)}, u32[]{:S(2)}) collective-permute-start(f32[512,256]{1,0:T(8,128)} %get-tuple-element.8.refs_0_), channel_id=1, source_target_pairs={{0,16},{8,24},{16,0},{24,8},{1,17},{9,25},{17,1},{25,9},{2,18},{10... | collective-permute-start | bytes 1572872 | tf_op jit(solution)/shard_map/ppermute | solution.py:353
  6.5 34.2 %collective-permute-start.9 = (f32[512,256]{1,0:T(8,128)}, f32[512,256]{1,0:T(8,128)}, u32[]{:S(2)}, u32[]{:S(2)}) collective-permute-start(f32[512,256]{1,0:T(8,128)} %get-tuple-element.8.refs_0_), channel_id=1, source_target_pairs={{0,8},{8,0},{16,24},{24,16},{1,9},{9,1},{17,25},{25,17},{2,10},{10... | collective-permute-start | bytes 1572872 | tf_op jit(solution)/shard_map/ppermute | solution.py:353
  8.0 67.5 %collective-permute-start.6 = (f32[512,256]{1,0:T(8,128)}, f32[512,256]{1,0:T(8,128)}, u32[]{:S(2)}, u32[]{:S(2)}) collective-permute-start(f32[512,256]{1,0:T(8,128)} %get-tuple-element.9.refs_0_), channel_id=1, source_target_pairs={{0,8},{8,0},{16,24},{24,16},{1,9},{9,1},{17,25},{25,17},{2,10},{10... | collective-permute-start | bytes 1572872 | tf_op jit(solution)/shard_map/ppermute | solution.py:353
  8.5 69.1 %collective-permute-start.7 = (f32[512,256]{1,0:T(8,128)}, f32[512,256]{1,0:T(8,128)}, u32[]{:S(2)}, u32[]{:S(2)}) collective-permute-start(f32[512,256]{1,0:T(8,128)} %get-tuple-element.9.refs_0_), channel_id=1, source_target_pairs={{0,16},{8,24},{16,0},{24,8},{1,17},{9,25},{17,1},{25,9},{2,18},{10... | collective-permute-start | bytes 1572872 | tf_op jit(solution)/shard_map/ppermute | solution.py:353
  8.6 71.1 %collective-permute-start.4 = (f32[512,256]{1,0:T(8,128)S(1)}, f32[512,256]{1,0:T(8,128)}, u32[]{:S(2)}, u32[]{:S(2)}) collective-permute-start(f32[512,256]{1,0:T(8,128)S(1)} %get-tuple-element.10.refs_0_), channel_id=1, source_target_pairs={{0,16},{8,24},{16,0},{24,8},{1,17},{9,25},{17,1},{25,9},{2,18},{10... | collective-permute-start | bytes 1572872 | tf_op jit(solution)/shard_map/ppermute | solution.py:353
  11.3 1.2 copy-start.2
  12.6 24.8 %copy-start.11 = (s32[64]{0:T(128)S(1)}, s32[64]{0:T(128)}, u32[]{:S(2)}) copy-start(s32[64]{0:T(128)} %param.13) | copy-start | bytes 772
  33.3 2.0 %copy-start.4 = (bf16[1024,2048]{1,0:T(8,128)(2,1)}, bf16[1024,2048]{1,0:T(8,128)(2,1)S(1)}, u32[]{:S(2)}) copy-start(bf16[1024,2048]{1,0:T(8,128)(2,1)S(1)} %get-tuple-element.5.dense_high) | copy-start | bytes 12582916
  35.3 2.0 %copy-start.6 = (bf16[1024,2048]{1,0:T(8,128)(2,1)}, bf16[1024,2048]{1,0:T(8,128)(2,1)S(1)}, u32[]{:S(2)}) copy-start(bf16[1024,2048]{1,0:T(8,128)(2,1)S(1)} %get-tuple-element.6.dense_low) | copy-start | bytes 12582916
  37.3 4.2 %copy-start.9 = (f32[8,8,8]{2,1,0:T(8,128)S(1)}, f32[8,8,8]{2,1,0:T(8,128)}, u32[]{:S(2)}) copy-start(f32[8,8,8]{2,1,0:T(8,128)} %param.14) | copy-start | bytes 6148
  37.3 4.4 %copy-start = (f32[1024,256]{1,0:T(8,128)S(1)}, f32[1024,256]{1,0:T(8,128)}, u32[]{:S(2)}) copy-start(f32[1024,256]{1,0:T(8,128)} %param.15) | copy-start | bytes 3145732
  39.1 41.2 %collective-permute-start = (f32[512,256]{1,0:T(8,128)S(1)}, f32[512,256]{1,0:T(8,128)S(1)}, u32[]{:S(2)}, u32[]{:S(2)}) collective-permute-start(f32[512,256]{1,0:T(8,128)S(1)} %get-tuple-element.11.refs_0_), channel_id=1, source_target_pairs={{0,8},{8,0},{16,24},{24,16},{1,9},{9,1},{17,25},{25,17},{2,10},{10... | collective-permute-start | bytes 1572872 | tf_op jit(solution)/shard_map/ppermute | solution.py:353
  40.7 40.7 %collective-permute-start.11 = (f32[512,256]{1,0:T(8,128)}, f32[512,256]{1,0:T(8,128)}, u32[]{:S(2)}, u32[]{:S(2)}) collective-permute-start(f32[512,256]{1,0:T(8,128)} %collective-permute-done.10.refs_2_), channel_id=1, source_target_pairs={{0,8},{8,0},{16,24},{24,16},{1,9},{9,1},{17,25},{25,17},{2,10},{10... | collective-permute-start | bytes 1572872 | tf_op jit(solution)/shard_map/ppermute | solution.py:358
  75.5 14.8 %collective-permute-start.8 = (f32[512,256]{1,0:T(8,128)}, f32[512,256]{1,0:T(8,128)S(1)}, u32[]{:S(2)}, u32[]{:S(2)}) collective-permute-start(f32[512,256]{1,0:T(8,128)} %collective-permute-done.6.refs_1_), channel_id=1, source_target_pairs={{0,16},{8,24},{16,0},{24,8},{1,17},{9,25},{17,1},{25,9},{2,18},{10... | collective-permute-start | bytes 1572872 | tf_op jit(solution)/shard_map/ppermute | solution.py:358
  77.6 4.3 %copy-start.8 = (f32[128,8,256]{2,0,1:T(8,128)S(1)}, f32[128,8,256]{2,0,1:T(8,128)}, u32[]{:S(2)}) copy-start(f32[128,8,256]{2,0,1:T(8,128)} %fusion.3) | copy-start | bytes 3145732
  77.6 15.9 %collective-permute-start.3 = (f32[512,256]{1,0:T(8,128)S(1)}, f32[512,256]{1,0:T(8,128)S(1)}, u32[]{:S(2)}, u32[]{:S(2)}) collective-permute-start(f32[512,256]{1,0:T(8,128)S(1)} %get-tuple-element.10.refs_0_), channel_id=1, source_target_pairs={{0,8},{8,0},{16,24},{24,16},{1,9},{9,1},{17,25},{25,17},{2,10},{10... | collective-permute-start | bytes 1572872 | tf_op jit(solution)/shard_map/ppermute | solution.py:353
  79.7 28.7 %collective-permute-start.1 = (f32[512,256]{1,0:T(8,128)S(1)}, f32[512,256]{1,0:T(8,128)S(1)}, u32[]{:S(2)}, u32[]{:S(2)}) collective-permute-start(f32[512,256]{1,0:T(8,128)S(1)} %get-tuple-element.11.refs_0_), channel_id=1, source_target_pairs={{0,16},{8,24},{16,0},{24,8},{1,17},{9,25},{17,1},{25,9},{2,18},{10... | collective-permute-start | bytes 1572872 | tf_op jit(solution)/shard_map/ppermute | solution.py:353
  80.3 23.1 %collective-permute-start.5 = (f32[512,256]{1,0:T(8,128)}, f32[512,256]{1,0:T(8,128)S(1)}, u32[]{:S(2)}, u32[]{:S(2)}) collective-permute-start(f32[512,256]{1,0:T(8,128)} %collective-permute-done.4.refs_2_), channel_id=1, source_target_pairs={{0,8},{8,0},{16,24},{24,16},{1,9},{9,1},{17,25},{25,17},{2,10},{10... | collective-permute-start | bytes 1572872 | tf_op jit(solution)/shard_map/ppermute | solution.py:358
  81.4 31.4 %collective-permute-start.2 = (f32[512,256]{1,0:T(8,128)S(1)}, f32[512,256]{1,0:T(8,128)S(1)}, u32[]{:S(2)}, u32[]{:S(2)}) collective-permute-start(f32[512,256]{1,0:T(8,128)S(1)} %collective-permute-done.refs_1_), channel_id=1, source_target_pairs={{0,16},{8,24},{16,0},{24,8},{1,17},{9,25},{17,1},{25,9},{2,18},{10... | collective-permute-start | bytes 1572872 | tf_op jit(solution)/shard_map/ppermute | solution.py:358
  90.4 32.7 %collective-permute-start.13 = (f32[16,32,256]{2,1,0:T(8,128)S(1)}, f32[16,32,256]{2,1,0:T(8,128)S(1)}, u32[]{:S(2)}, u32[]{:S(2)}) collective-permute-start(f32[16,32,256]{2,1,0:T(8,128)S(1)} %bitcast.29), channel_id=1, source_target_pairs={{0,1},{1,2},{2,3},{3,4},{4,5},{5,6},{6,7},{7,0},{8,9},{9,10},{10,1... | collective-permute-start | bytes 1572872 | tf_op jit(solution)/shard_map/ppermute | solution.py:400
  91.0 25.8 %copy-start.7 = (bf16[1024,2048]{1,0:T(8,128)(2,1)S(1)}, bf16[1024,2048]{1,0:T(8,128)(2,1)}, u32[]{:S(2)}) copy-start(bf16[1024,2048]{1,0:T(8,128)(2,1)} %copy-done.6) | copy-start | bytes 12582916
  93.5 29.5 %collective-permute-start.12 = (f32[16,32,256]{2,1,0:T(8,128)S(1)}, f32[16,32,256]{2,1,0:T(8,128)S(1)}, u32[]{:S(2)}, u32[]{:S(2)}) collective-permute-start(f32[16,32,256]{2,1,0:T(8,128)S(1)} %bitcast.31), channel_id=1, source_target_pairs={{0,1},{1,2},{2,3},{3,4},{4,5},{5,6},{6,7},{7,0},{8,9},{9,10},{10,1... | collective-permute-start | bytes 1572872 | tf_op jit(solution)/shard_map/ppermute | solution.py:400
  103.4 13.3 %copy-start.5 = (bf16[1024,2048]{1,0:T(8,128)(2,1)S(1)}, bf16[1024,2048]{1,0:T(8,128)(2,1)}, u32[]{:S(2)}) copy-start(bf16[1024,2048]{1,0:T(8,128)(2,1)} %copy-done.4) | copy-start | bytes 12582916
  105.8 11.0 %copy-start.10 = (f32[2,32,32]{2,1,0:T(8,128)S(1)}, f32[2,32,32]{2,1,0:T(8,128)}, u32[]{:S(2)}) copy-start(f32[2,32,32]{2,1,0:T(8,128)} %param.9) | copy-start | bytes 24580
  105.8 17.2 %collective-permute-start.15 = (f32[16,32,256]{2,1,0:T(8,128)S(1)}, f32[16,32,256]{2,1,0:T(8,128)S(1)}, u32[]{:S(2)}, u32[]{:S(2)}) collective-permute-start(f32[16,32,256]{2,1,0:T(8,128)S(1)} %bitcast.33), channel_id=1, source_target_pairs={{1,0},{2,1},{3,2},{4,3},{5,4},{6,5},{7,6},{0,7},{9,8},{10,9},{11,1... | collective-permute-start | bytes 1572872 | tf_op jit(solution)/shard_map/ppermute | solution.py:399
  114.1 9.4 %collective-permute-start.14 = (f32[16,32,256]{2,1,0:T(8,128)S(1)}, f32[16,32,256]{2,1,0:T(8,128)S(1)}, u32[]{:S(2)}, u32[]{:S(2)}) collective-permute-start(f32[16,32,256]{2,1,0:T(8,128)S(1)} %bitcast.35), channel_id=1, source_target_pairs={{1,0},{2,1},{3,2},{4,3},{5,4},{6,5},{7,6},{0,7},{9,8},{10,9},{11,1... | collective-permute-start | bytes 1572872 | tf_op jit(solution)/shard_map/ppermute | solution.py:399

commit v3 on v0

v3 whole, which is shorter than its diff:
```python
import functools

import jax
import jax.numpy as jnp
from jax import lax
from jax.experimental import pallas as pl
from jax.experimental.pallas import tpu as pltpu
from jax.sharding import PartitionSpec as P

LANES = 128
SUB = 8


def split(x):
    high = x.astype(jnp.bfloat16)
    low = (x - high.astype(jnp.float32)).astype(jnp.bfloat16)
    return high, low


def split_outside(x):
    high = lax.reduce_precision(x, exponent_bits=8, mantissa_bits=7)
    return high.astype(jnp.bfloat16), (x - high).astype(jnp.bfloat16)


def dot3(a, b, dims=(((1,), (0,)), ((), ()))):
    a_high, a_low = a
    b_high, b_low = b
    dot = functools.partial(lax.dot_general, dimension_numbers=dims, preferred_element_type=jnp.float32)
    return dot(a_high, b_high) + (dot(a_high, b_low) + dot(a_low, b_high))


def owner_rows(atom_ids, atom_owner):
    match = atom_ids[..., None] == jnp.arange(atom_owner.shape[0], dtype=jnp.int32)
    found_rows = jnp.sum(jnp.where(match, atom_owner, 0), axis=-1)
    return jnp.where(atom_ids >= 0, found_rows, -1)


def fused_kernel(
    cells_ref, values_ref, field_ref, keys_ref, coupling_ref, mats_ref,
    rot_ref, before_ref, after_ref, far_ref,
    dense_high, dense_low, field_high, field_low, partials, select, sums, arrived, mine, others,
    returned, one, two, three,
    send_one, recv_one, send_two, recv_two, send_three, recv_three,
    send_sums, recv_sums, send_mine, recv_mine, send_out, recv_out,
    send_before, recv_before, send_after, recv_after,
):
    entries, proj, tile = values_ref.shape
    groups = dense_high.shape[1] // LANES
    items, rows, bands = rot_ref.shape
    sides = before_ref.shape[0]
    dom_count, own, _ = sums.shape
    band_count = mats_ref.shape[0]
    dom, band = lax.axis_index("dom"), lax.axis_index("band")
    mesh_id = pl.DeviceIdType.MESH
    barrier = pltpu.get_barrier_semaphore()
    flip_one = band + 1 - 2 * lax.rem(band, 2)
    flip_two = lax.rem(band + 2, band_count)
    flip_three = lax.rem(flip_one + 2, band_count)

    def dom_peer(k):
        return lax.rem(dom + k, dom_count)

    def band_peer(k):
        return lax.rem(band + k, band_count)

    def remote(src, dst, send, recv, target):
        return pltpu.make_async_remote_copy(
            src_ref=src, dst_ref=dst, send_sem=send, recv_sem=recv,
            device_id=target, device_id_type=mesh_id,
        )

    def greet(k, carry):
        pl.semaphore_signal(barrier, inc=1, device_id={"dom": dom_peer(k)}, device_id_type=mesh_id)
        return carry

    lax.fori_loop(1, dom_count, greet, 0)
    for k in range(1, band_count):
        pl.semaphore_signal(barrier, inc=1, device_id={"band": band_peer(k)}, device_id_type=mesh_id)
    pl.semaphore_wait(barrier, dom_count - 1 + band_count - 1)

    def own_rows(i):
        return field_ref.at[pl.ds(i * rows, rows)]

    def one_copy(i):
        return remote(own_rows(i), one.at[i], send_one.at[i], recv_one.at[i], {"band": flip_one})

    def two_copy(i):
        return remote(own_rows(i), two.at[i], send_two.at[i], recv_two.at[i], {"band": flip_two})

    def three_copy(i):
        if i % 2 == 0:
            return remote(one.at[i], three.at[i], send_three.at[i], recv_three.at[i], {"band": flip_two})
        return remote(two.at[i], three.at[i], send_three.at[i], recv_three.at[i], {"band": flip_one})

    def forward(i):
        (one_copy if i % 2 == 0 else two_copy)(i).wait_recv()
        three_copy(i).start()

    for i in range(items):
        one_copy(i).start()
        two_copy(i).start()

    field_high[...], field_low[...] = split(field_ref[...])
    lane_ids = lax.broadcasted_iota(jnp.int32, (LANES, tile), 0)

    def dense_row(e):
        cells = cells_ref[pl.ds(e, 1), :]
        group = jnp.broadcast_to(cells // LANES, (proj, tile))
        spot = jnp.broadcast_to(cells % LANES, (LANES, tile))
        hot = jnp.where(spot == lane_ids, 1.0, 0.0).astype(jnp.bfloat16)
        values = values_ref[e]
        high = values.astype(jnp.bfloat16).astype(jnp.float32)
        low = values - high
        parts = [jnp.where(group == g, high, 0.0) for g in range(groups)]
        parts += [jnp.where(group == g, low, 0.0) for g in range(groups)]
        left = jnp.concatenate(parts, axis=0).astype(jnp.bfloat16)
        out = lax.dot_general(
            left, hot, (((1,), (1,)), ((), ())), preferred_element_type=jnp.float32
        )
        total = out[: groups * proj] + out[groups * proj :]
        return jnp.concatenate([total[g * proj : (g + 1) * proj] for g in range(groups)], axis=1)

    def pair(i, carry):
        both = jnp.concatenate([dense_row(2 * i), dense_row(2 * i + 1)], axis=0)
        at = pl.ds(pl.multiple_of(i * 2 * proj, 2 * proj), 2 * proj)
        dense_high[at, :], dense_low[at, :] = split(both)
        return carry

    block = 256

    def product(i, carry):
        at = pl.ds(pl.multiple_of(i * block, block), block)
        partials[at, :] = dot3(
            (dense_high[at, :], dense_low[at, :]), (field_high[...], field_low[...])
        )
        return carry

    pairs = entries // 2
    lax.fori_loop(0, pairs // 2, pair, 0)
    forward(0)
    lax.fori_loop(pairs // 2, pairs, pair, 0)
    lax.fori_loop(0, entries * proj // block, product, 0)
    forward(1)

    partial_high, partial_low = split(partials[...])

    def gather_sums(d, carry):
        ids = d * own + lax.broadcasted_iota(jnp.int32, (own, entries * proj), 0)
        hit = jnp.where(ids == keys_ref[...], 1.0, 0.0).astype(jnp.bfloat16)
        select[pl.ds(pl.multiple_of(d * own, own), own), :] = hit
        sums[d] = jnp.dot(hit, partial_high, preferred_element_type=jnp.float32) + jnp.dot(
            hit, partial_low, preferred_element_type=jnp.float32
        )
        return carry

    lax.fori_loop(0, dom_count, gather_sums, 0)

    def sums_copy(k):
        return remote(
            sums.at[dom_peer(k)], arrived.at[k], send_sums.at[k], recv_sums.at[k], {"dom": dom_peer(k)}
        )

    def mine_copy(k):
        return remote(mine, others.at[k], send_mine.at[k], recv_mine.at[k], {"band": band_peer(k)})

    def start_sums(k, carry):
        sums_copy(k).start()
        return carry

    def add(k, total):
        sums_copy(k).wait_recv()
        return total + arrived[k]

    lax.fori_loop(1, dom_count, start_sums, 0)
    total = lax.fori_loop(1, dom_count, add, sums[dom])
    mine[...] = dot3(split(coupling_ref[...]), split(total))
    for k in range(1, band_count):
        mine_copy(k).start()
    forward(2)
    result = dot3(split(mine[...]), split(mats_ref[band]))
    for k in range(1, band_count):
        mine_copy(k).wait_recv()
        source = lax.rem(band - k + band_count, band_count)
        result = result + dot3(split(others[k]), split(mats_ref[source]))
    returned[dom] = result

    def start_out(k, carry):
        remote(
            returned.at[dom], returned.at[dom], send_out.at[k], recv_out.at[k], {"dom": dom_peer(k)}
        ).start()
        return carry

    lax.fori_loop(1, dom_count, start_out, 0)
    for i in range(3, items):
        forward(i)

    def after_copy(i):
        return remote(
            rot_ref.at[i], after_ref.at[i], send_after.at[i], recv_after.at[i],
            {"dom": dom_peer(dom_count - 1)},
        )

    def before_copy(i):
        return remote(
            rot_ref.at[items - sides + i], before_ref.at[i], send_before.at[i], recv_before.at[i],
            {"dom": dom_peer(1)},
        )

    def rotate(i):
        (two_copy if i % 2 == 0 else one_copy)(i).wait_recv()
        three_copy(i).wait_recv()
        out = dot3(split(own_rows(i)[...]), split(mats_ref[band]))
        out = out + dot3(split(one[i]), split(mats_ref[flip_one]))
        out = out + dot3(split(two[i]), split(mats_ref[flip_two]))
        rot_ref[i] = out + dot3(split(three[i]), split(mats_ref[flip_three]))
        if i < sides:
            after_copy(i).start()
        if i >= items - sides:
            before_copy(i - (items - sides)).start()

    def finish_out(k, carry):
        source = lax.rem(dom - k + dom_count, dom_count)
        remote(
            returned.at[dom], returned.at[source], send_out.at[k], recv_out.at[k], {"dom": dom_peer(k)}
        ).wait()
        sums_copy(k).wait_send()
        return carry

    transposed = (((0,), (0,)), ((), ()))

    def far_sum():
        lax.fori_loop(1, dom_count, finish_out, 0)
        all_rows = returned[...].reshape(dom_count * own, bands)
        high, low = split(all_rows)
        back = lax.dot_general(
            select[...], high, transposed, preferred_element_type=jnp.float32
        ) + lax.dot_general(select[...], low, transposed, preferred_element_type=jnp.float32)
        back = split(back)
        for c in range(0, far_ref.shape[0], block):
            far_ref[c : c + block, :] = dot3(
                (dense_high[:, c : c + block], dense_low[:, c : c + block]), back, transposed
            )

    far_at = min(1, items - 1)
    for i in range(items):
        rotate(i)
        if i == far_at:
            far_sum()
    for i in range(sides):
        after_copy(i).wait()
        before_copy(i).wait()
    for i in range(items):
        one_copy(i).wait_send()
        two_copy(i).wait_send()
        three_copy(i).wait_send()
    for k in range(1, band_count):
        mine_copy(k).wait_send()


def fused(tile_cells, projectors, field, keys, coupling, mats, items, sides, dom_count):
    entries, proj, _ = projectors.shape
    cell_count, bands = field.shape
    band_count = mats.shape[0]
    own = coupling.shape[0]
    rows = cell_count // items
    vmem = pl.BlockSpec(memory_space=pltpu.VMEM)
    dma = pltpu.SemaphoreType.DMA
    f32, bf16 = jnp.float32, jnp.bfloat16
    return pl.pallas_call(
        fused_kernel,
        in_specs=[vmem] * 6,
        out_specs=[vmem] * 4,
        out_shape=[
            jax.ShapeDtypeStruct((items, rows, bands), f32),
            jax.ShapeDtypeStruct((sides, rows, bands), f32),
            jax.ShapeDtypeStruct((sides, rows, bands), f32),
            jax.ShapeDtypeStruct((cell_count, bands), f32),
        ],
        scratch_shapes=[
            pltpu.VMEM((entries * proj, cell_count), bf16),
            pltpu.VMEM((entries * proj, cell_count), bf16),
            pltpu.VMEM((cell_count, bands), bf16),
            pltpu.VMEM((cell_count, bands), bf16),
            pltpu.VMEM((entries * proj, bands), f32),
            pltpu.VMEM((dom_count * own, entries * proj), bf16),
            pltpu.VMEM((dom_count, own, bands), f32),
            pltpu.VMEM((dom_count, own, bands), f32),
            pltpu.VMEM((own, bands), f32),
            pltpu.VMEM((band_count, own, bands), f32),
            pltpu.VMEM((dom_count, own, bands), f32),
            pltpu.VMEM((items, rows, bands), f32),
            pltpu.VMEM((items, rows, bands), f32),
            pltpu.VMEM((items, rows, bands), f32),
        ]
        + [dma((items,))] * 6
        + [dma((dom_count,))] * 2
        + [dma((band_count,))] * 2
        + [dma((dom_count,))] * 2
        + [dma((sides,))] * 4,
        compiler_params=pltpu.CompilerParams(
            vmem_limit_bytes=60 * 2**20, collective_id=0, has_side_effects=True
        ),
        name="fused",
    )(tile_cells, projectors, field, keys, coupling, mats)


def local_kernel(field_ref, before_ref, after_ref, weight_ref, far_ref, first_ref, second_ref):
    planes = first_ref.shape[0]
    for p in range(planes):
        here = field_ref[p]
        first_ref[p] = here
        low = before_ref[...] if p == 0 else field_ref[p - 1]
        high = after_ref[...] if p == planes - 1 else field_ref[p + 1]
        beside = low + high
        beside = beside + jnp.roll(here, 1, 0) + jnp.roll(here, -1, 0)
        beside = beside + jnp.roll(here, 1, 1) + jnp.roll(here, -1, 1)
        second_ref[p] = weight_ref[p] * here - 0.5 * beside + far_ref[p]


def local_apply(field, before, after, weight, far):
    planes, ny, nz, bands = far.shape
    whole = pl.BlockSpec((planes, ny, nz, LANES), lambda i: (0, 0, 0, i))
    side = pl.BlockSpec((ny, nz, LANES), lambda i: (0, 0, i))
    return pl.pallas_call(
        local_kernel,
        grid=(bands // LANES,),
        in_specs=[whole, side, side]
        + [pl.BlockSpec((planes, ny, nz, LANES), lambda i: (0, 0, 0, 0)), whole],
        out_specs=[whole, whole],
        out_shape=[jax.ShapeDtypeStruct(far.shape, jnp.float32)] * 2,
        compiler_params=pltpu.CompilerParams(vmem_limit_bytes=40 * 2**20),
        name="local",
    )(field, before, after, weight, far)


def body(orbitals, potential, projectors, tile_cells, tile_atom, atom_owner, coupling, rotation):
    planes, ny, nz, bands = orbitals.shape
    cell_count = planes * ny * nz
    entries, proj, _ = projectors.shape
    atom_total = atom_owner.shape[0]
    dom_count = lax.axis_size("dom")
    domain_index = lax.axis_index("dom")
    field = orbitals.reshape(cell_count, bands)
    sides = 2
    band_mats = rotation.reshape(-1, bands, bands)
    my_atoms = lax.dynamic_slice_in_dim(tile_atom, domain_index * entries, entries)
    my_rows = owner_rows(my_atoms, atom_owner)
    keys = (my_rows[:, None] * proj + jnp.arange(proj, dtype=jnp.int32)).reshape(1, -1)
    own = coupling.shape[0]
    eye = jnp.eye(own, dtype=bool)[:, None, :, None]
    coupled = jnp.where(eye, coupling[:, :, None, :], 0.0).reshape(own * proj, own * proj)
    rotated, before, after, far = fused(
        tile_cells, projectors, field, keys, coupled, band_mats, planes * sides, sides, dom_count
    )
    weight = jnp.broadcast_to((3.0 + potential)[..., None], (planes, ny, nz, LANES))
    first, second = local_apply(
        rotated.reshape(orbitals.shape),
        before.reshape(ny, nz, bands),
        after.reshape(ny, nz, bands),
        weight,
        far.reshape(orbitals.shape),
    )
    return first, second


def solution(mesh):
    return jax.shard_map(
        body,
        mesh=mesh,
        in_specs=(
            P("dom", None, None, "band"),
            P("dom", None, None),
            P("dom", None, None),
            P("dom", None),
            P(),
            P(),
            P("dom", None, None),
            P(None, "band"),
        ),
        out_specs=(P("dom", None, None, "band"), P("dom", None, None, "band")),
        check_vma=False,
    )
```

time: 326 us -> 131 us (0.40)
  matrix products: 144 us -> 0 us
  waiting for transfers between devices: 121 us -> 0 us
  Pallas kernels: 0 us -> 118 us
  blocking collectives: 15.2 us -> 0 us
  between operations: 15.6 us -> 0.67 us
  local copies, waits for them, and re-layouts: 22.8 us -> 8.15 us
  starting transfers between devices: 4.61 us -> 0 us
    dot_general x15 -> x0, matrix products: 144 us -> none  [the longest x8 98.7 us: densify(): jnp.einsum('ekt,etc->ekc', values, one_hot, precision=lax.Precision.HIGHEST)]
    pallas_call x0 -> x2, Pallas kernels: none -> 118 us  [the longest x1 116 us: fused(): pl.pallas_call(fused_kernel, in_specs=[vmem] * 6, out_specs=[vmem] * 4, o...]
    all_gather x2 -> x0, waiting for transfers between devices: 106 us -> none  [the longest x1 79.7 us: body(): lax.all_gather(applied, 'band', axis=3, tiled=True)]
    all_gather x1 -> x0, blocking collectives: 15.2 us -> none  [body(): lax.all_gather(scaled, 'dom', axis=0, tiled=True)]
    reduce_scatter x1 -> x0, waiting for transfers between devices: 14.9 us -> none  [body(): lax.psum_scatter(jnp.einsum('ea,ekb->akb', columns, partials, precision=l...]
    dot_general x1 -> x0, local copies, waits for them, and re-layouts: 9.54 us -> none  [body(): jnp.einsum('rc,rb->cb', dense_proj, returned_rows, precision=lax.Precisio...]
    slice x5 -> x0, local copies, waits for them, and re-layouts: 6.52 us -> none  [the longest x2 2.52 us: body(): beside = beside + jnp.roll(orbitals, 1, 2) + jnp.roll(orbitals, -1, 2)]
    eq x8 -> x0, local copies, waits for them, and re-layouts: 5.9 us -> none  [densify(): one_hot = (tile_index[..., None] == cell_ids).astype(jnp.float32)]
  transfers between devices with their start and end apart: 5 -> 0, of which waited for: 3 -> 0; matrix products, arithmetic and copies ran while one was open for 13% -> 0% of each run, Pallas kernels for 0% -> 0%
where the time goes in v3:
time: 131 us; the launch traced here: 130 us
  Pallas kernels  118 us (90%)
  local copies, waits for them, and re-layouts  8.15 us (6%)
  other arithmetic  3.2 us (2%)
    pallas_call x1, Pallas kernels, fused(): pl.pallas_call(fused_kernel, in_specs=[vmem] * 6, out_specs=[vmem] * 4, o...  116 us
    unnamed x8, local copies, waits for them, and re-layouts  5.62 us
    pallas_call x1, Pallas kernels, local_apply(): pl.pallas_call(local_kernel, grid=(bands // LANES,), in_specs=[whole, sid...  2.87 us

profile of v3, /device:TPU:0, one launch (start us, length us, event | category | flops | bytes accessed | tf_op | source)
XLA Modules:
  0.0 130.5 jit_solution(5556919189326730670)
XLA Ops:
  0.6 0.8 dynamic_slice.3
  1.4 0.7 select_reduce_fusion
  2.1 0.8 fusion
  2.9 0.8 broadcast_add_fusion
  3.7 0.1 iota_add_fusion
  3.8 0.7 add.36.keys_ref
  4.5 0.8 broadcast_select_fusion
  5.3 0.7 select_n.23.coupling_ref
  6.0 0.3 broadcast_in_dim.50.weight_ref
  6.4 115.6 %fused.1 = (f32[4,512,256]{2,1,0:T(8,128)}, f32[2,512,256]{2,1,0:T(8,128)}, f32[2,512,256]{2,1,0:T(8,128)}, f32[2048,256]{1,0:T(8,128)}) custom-call(s32[128,256]{1,0:T(8,128)} %cells_ref.1, f32[128,8,256]{2,1,0:T(8,128)} %values_ref.1, f32[2048,256]{1,0:T(8,128)} %bitcast.12, s32[1,1024]{1,0:T(1,128)} %add.36.keys_ref, f32[64,64]{1,0:T(8,128)} %select_n.23.coupling_ref, ...), custom_call_target="tpu_custom_call" | custom-call | tf_op jit(solution)/shard_map/fused/pallas_call | solution.py:269
  122.0 0.0 copy-start
  122.0 1.6 %copy-done = f32[4,512,256]{2,1,0:T(8,128)S(1)} copy-done((f32[4,512,256]{2,1,0:T(8,128)S(1)}, f32[4,512,256]{2,1,0:T(8,128)}, u32[]{:S(2)}) %copy-start) | copy-done | bytes 2097176
  123.6 0.0 copy-start.1
  123.6 1.6 %copy-done.1 = f32[2048,256]{1,0:T(8,128)S(1)} copy-done((f32[2048,256]{1,0:T(8,128)S(1)}, f32[2048,256]{1,0:T(8,128)}, u32[]{:S(2)}) %copy-start.1) | copy-done | bytes 2097176
  125.2 0.0 copy-start.2
  125.2 1.2 copy-done.2
  126.4 0.0 copy-start.3
  126.4 1.2 copy-done.3
  127.6 2.9 %local.1 = (f32[2,32,32,256]{3,2,1,0:T(8,128)}, f32[2,32,32,256]{3,2,1,0:T(8,128)}) custom-call(f32[2,32,32,256]{3,2,1,0:T(8,128)S(1)} %bitcast.8, f32[32,32,256]{2,1,0:T(8,128)S(1)} %bitcast.10, f32[32,32,256]{2,1,0:T(8,128)S(1)} %bitcast.11, f32[2,32,32,128]{3,2,1,0:T(8,128)S(1)} %broadcast_in_dim.50.weight_ref, f32[2,32,32,256]{3,2,1,0:T(8,128)S(1)} %bitcast.9), custom_call_target="tpu_custom_call" | custom-call | tf_op jit(solution)/shard_map/local/pallas_call | solution.py:324
  (1 shorter events, 0.0 us)
Async XLA Ops:
  122.0 1.6 %copy-start = (f32[4,512,256]{2,1,0:T(8,128)S(1)}, f32[4,512,256]{2,1,0:T(8,128)}, u32[]{:S(2)}) copy-start(f32[4,512,256]{2,1,0:T(8,128)} %get-tuple-element.6) | copy-start | bytes 6291460
  123.6 1.6 %copy-start.1 = (f32[2048,256]{1,0:T(8,128)S(1)}, f32[2048,256]{1,0:T(8,128)}, u32[]{:S(2)}) copy-start(f32[2048,256]{1,0:T(8,128)} %get-tuple-element.9) | copy-start | bytes 6291460
  125.2 1.2 copy-start.2
  126.4 1.2 copy-start.3

commit v4 on v3

--- a/solution.py
+++ b/solution.py
@@ -172,17 +172,12 @@
         return total + arrived[k]
 
     lax.fori_loop(1, dom_count, start_sums, 0)
+    for i in range(2, items):
+        forward(i)
     total = lax.fori_loop(1, dom_count, add, sums[dom])
     mine[...] = dot3(split(coupling_ref[...]), split(total))
     for k in range(1, band_count):
         mine_copy(k).start()
-    forward(2)
-    result = dot3(split(mine[...]), split(mats_ref[band]))
-    for k in range(1, band_count):
-        mine_copy(k).wait_recv()
-        source = lax.rem(band - k + band_count, band_count)
-        result = result + dot3(split(others[k]), split(mats_ref[source]))
-    returned[dom] = result
 
     def start_out(k, carry):
         remote(
@@ -190,9 +185,14 @@
         ).start()
         return carry
 
-    lax.fori_loop(1, dom_count, start_out, 0)
-    for i in range(3, items):
-        forward(i)
+    def return_sums():
+        result = dot3(split(mine[...]), split(mats_ref[band]))
+        for k in range(1, band_count):
+            mine_copy(k).wait_recv()
+            source = lax.rem(band - k + band_count, band_count)
+            result = result + dot3(split(others[k]), split(mats_ref[source]))
+        returned[dom] = result
+        lax.fori_loop(1, dom_count, start_out, 0)
 
     def after_copy(i):
         return remote(
@@ -241,11 +241,11 @@
                 (dense_high[:, c : c + block], dense_low[:, c : c + block]), back, transposed
             )
 
-    far_at = min(1, items - 1)
-    for i in range(items):
+    rotate(0)
+    return_sums()
+    for i in range(1, items):
         rotate(i)
-        if i == far_at:
-            far_sum()
+    far_sum()
     for i in range(sides):
         after_copy(i).wait()
         before_copy(i).wait()
@@ -266,6 +266,9 @@
     vmem = pl.BlockSpec(memory_space=pltpu.VMEM)
     dma = pltpu.SemaphoreType.DMA
     f32, bf16 = jnp.float32, jnp.bfloat16
+    dense_bytes = 4 * entries * proj * (cell_count + bands)
+    sums_bytes = 12 * dom_count * own * bands + 2 * dom_count * own * entries * proj
+    scratch_bytes = dense_bytes + sums_bytes + 16 * cell_count * bands
     return pl.pallas_call(
         fused_kernel,
         in_specs=[vmem] * 6,
@@ -298,7 +301,7 @@
         + [dma((dom_count,))] * 2
         + [dma((sides,))] * 4,
         compiler_params=pltpu.CompilerParams(
-            vmem_limit_bytes=60 * 2**20, collective_id=0, has_side_effects=True
+            vmem_limit_bytes=min(60 * 2**20, scratch_bytes + sums_bytes // 2 + 12 * 2**20), collective_id=0, has_side_effects=True
         ),
         name="fused",
     )(tile_cells, projectors, field, keys, coupling, mats)
@@ -328,7 +331,7 @@
         + [pl.BlockSpec((planes, ny, nz, LANES), lambda i: (0, 0, 0, 0)), whole],
         out_specs=[whole, whole],
         out_shape=[jax.ShapeDtypeStruct(far.shape, jnp.float32)] * 2,
-        compiler_params=pltpu.CompilerParams(vmem_limit_bytes=40 * 2**20),
+        compiler_params=pltpu.CompilerParams(vmem_limit_bytes=20 * 2**20),
         name="local",
     )(field, before, after, weight, far)
 

time: 131 us -> 118 us (0.901)
  Pallas kernels: 118 us -> 108 us
  local copies, waits for them, and re-layouts: 8.15 us -> 5.12 us
    pallas_call x1, Pallas kernels: 116 us -> 105 us  [fused(): pl.pallas_call(fused_kernel, in_specs=[vmem] * 6, out_specs=[vmem] * 4, o...]
    unnamed x8, local copies, waits for them, and re-layouts: 5.62 us -> 3.72 us
where the time goes in v4:
time: 118 us; the launch traced here: 117 us
  Pallas kernels  108 us (92%)
  local copies, waits for them, and re-layouts  5.12 us (4%)
  other arithmetic  3.2 us (3%)
    pallas_call x1, Pallas kernels, fused(): pl.pallas_call(fused_kernel, in_specs=[vmem] * 6, out_specs=[vmem] * 4, o...  105 us
    unnamed x8, local copies, waits for them, and re-layouts  3.72 us
    pallas_call x1, Pallas kernels, local_apply(): pl.pallas_call(local_kernel, grid=(bands // LANES,), in_specs=[whole, sid...  2.94 us

profile of v4, /device:TPU:0, one launch (start us, length us, event | category | flops | bytes accessed | tf_op | source)
XLA Modules:
  0.0 116.7 jit_solution(15231345882693430066)
XLA Ops:
  0.6 0.0 copy-start.1
  0.6 0.8 dynamic_slice.3
  1.5 0.7 select_reduce_fusion
  2.2 0.8 fusion
  3.0 0.8 broadcast_add_fusion
  3.8 0.1 iota_add_fusion
  3.9 0.1 add.36.keys_ref
  4.0 0.8 broadcast_select_fusion
  4.8 0.1 select_n.23.coupling_ref
  4.9 0.3 broadcast_in_dim.50.weight_ref
  5.3 0.0 copy-done.1
  5.3 0.0 copy-start
  5.3 1.6 %copy-done = f32[2,32,32,256]{3,2,1,0:T(8,128)S(1)} copy-done((f32[2,32,32,256]{3,2,1,0:T(8,128)S(1)}, f32[2,32,32,256]{3,2,1,0:T(8,128)}, u32[]{:S(2)}) %copy-start) | copy-done | bytes 2097176
  6.9 0.0 copy-start.2
  6.9 1.2 %copy-done.2 = f32[1024,256]{1,0:T(8,128)S(1)} copy-done((f32[1024,256]{1,0:T(8,128)S(1)}, f32[1024,256]{1,0:T(8,128)}, u32[]{:S(2)}) %copy-start.2) | copy-done | bytes 1048600
  8.1 0.0 copy-start.3
  8.1 0.9 copy-done.3
  9.0 104.8 %fused.1 = (f32[4,512,256]{2,1,0:T(8,128)S(1)}, f32[2,512,256]{2,1,0:T(8,128)S(1)}, f32[2,512,256]{2,1,0:T(8,128)S(1)}, f32[2048,256]{1,0:T(8,128)S(1)}) custom-call(s32[128,256]{1,0:T(8,128)S(1)} %copy-done.3, f32[128,8,256]{2,1,0:T(8,128)S(1)} %copy-done.1, f32[2048,256]{1,0:T(8,128)S(1)} %bitcast.10, s32[1,1024]{1,0:T(1,128)S(1)} %add.36.keys_ref, ...), custom_call_target="tpu_custom_call" | custom-call | tf_op jit(solution)/shard_map/fused/pallas_call | solution.py:272
  113.8 2.9 %local.1 = (f32[2,32,32,256]{3,2,1,0:T(8,128)}, f32[2,32,32,256]{3,2,1,0:T(8,128)}) custom-call(f32[2,32,32,256]{3,2,1,0:T(8,128)S(1)} %bitcast.8, f32[32,32,256]{2,1,0:T(8,128)S(1)} %bitcast.12, f32[32,32,256]{2,1,0:T(8,128)S(1)} %bitcast.13, f32[2,32,32,128]{3,2,1,0:T(8,128)S(1)} %broadcast_in_dim.50.weight_ref, f32[2,32,32,256]{3,2,1,0:T(8,128)S(1)} %bitcast.9), custom_call_target="tpu_custom_call" | custom-call | tf_op jit(solution)/shard_map/local/pallas_call | solution.py:327
  (1 shorter events, 0.0 us)
Async XLA Ops:
  0.6 4.6 %copy-start.1 = (f32[128,8,256]{2,1,0:T(8,128)S(1)}, f32[128,8,256]{2,1,0:T(8,128)}, u32[]{:S(2)}) copy-start(f32[128,8,256]{2,1,0:T(8,128)} %values_ref.1) | copy-start | bytes 3145732
  5.3 1.6 %copy-start = (f32[2,32,32,256]{3,2,1,0:T(8,128)S(1)}, f32[2,32,32,256]{3,2,1,0:T(8,128)}, u32[]{:S(2)}) copy-start(f32[2,32,32,256]{3,2,1,0:T(8,128)} %param.8) | copy-start | bytes 6291460
  6.9 1.2 %copy-start.2 = (f32[1024,256]{1,0:T(8,128)S(1)}, f32[1024,256]{1,0:T(8,128)}, u32[]{:S(2)}) copy-start(f32[1024,256]{1,0:T(8,128)} %param.15) | copy-start | bytes 3145732
  8.1 0.9 copy-start.3
